TPU v7x, 128 devices: a whole 4x4x4 slice. The times are simulated.
128 devices in a mesh: seq: 32 (over x, y, core), blk: 4 (over z).
Axes of the slice: x: 4, y: 4, z: 4, core: 2. Of those that a mesh axis runs over, the one named last changes fastest.
Arguments:
- nodes: bfloat16 [16384, 1024], P(('seq', 'blk')), may hold values from -21 to 21
- w_qkv: bfloat16 [1024, 3072], replicated, may hold values from -0.1875 to 0.1875
- w_out: bfloat16 [1024, 1024], replicated, may hold values from -0.1875 to 0.1875
- perm: int32 [16384], P('seq'), may hold values from 0 to 16383, as said below
- blocks: int32 [128, 8], P('seq'), may hold values from 0 to 127, as said below
- grad_out: bfloat16 [16384, 1024], P(('seq', 'blk')), may hold values from -24 to 24
Outputs:
- out: bfloat16 [16384, 1024], P(('seq', 'blk'))
- grad_nodes: bfloat16 [16384, 1024], P(('seq', 'blk'))
- w_out_grad: float32 [1024, 1024], P(('seq', 'blk'))
Inputs may be any that keep to these rules, and one draw needn't show every extreme that they name: perm is a permutation that maps each aligned run of 512 positions onto itself. Within each aligned run of 4 rows (query blocks), at most 2 entries name blocks of any one aligned run of 4 key blocks; the run with the same index is named exactly 2 times, and one run, the same for all, is named exactly 2 times by every run of rows.
All inputs are finite; a program needn't handle non-finite values.
Results may differ from a plain program's by a relative error of at most 0.023.
The roundings to bfloat16 on the way count: a program that leaves them out, or rounds other values in their place, can miss the bound.
Values may be sent and summed in bfloat16 or wider, within the bound.
A program may use at most 128 MiB of HBM per device.

v0:
```python
import jax
import jax.numpy as jnp
from jax import lax
from jax.sharding import PartitionSpec as P

HDIM = 64


def plan_requests(flat_ids, group_blocks, seq_count, capacity):
    owner_group = flat_ids // group_blocks
    local_block = flat_ids % group_blocks
    positions = jnp.arange(flat_ids.shape[0], dtype=jnp.int32)
    before = (owner_group[:, None] == owner_group[None, :]) & (
        positions[None, :] < positions[:, None]
    )
    rank_index = jnp.sum(before.astype(jnp.int32), axis=1)
    slot_index = owner_group * capacity + rank_index
    slot_hits = (
        slot_index[:, None] == jnp.arange(seq_count * capacity, dtype=jnp.int32)[None, :]
    ).astype(jnp.int32)
    request = jnp.sum(slot_hits * local_block[:, None], axis=0).reshape(seq_count, capacity)
    return (slot_index, request)


def to_cluster(row_data, local_perm):
    return jnp.take(row_data, local_perm, axis=0)


def from_cluster(row_data, local_perm):
    return jnp.zeros_like(row_data).at[local_perm].set(row_data)


def on_device(nodes, w_qkv, w_out, perm, blocks, grad_out):
    node_dev, model_width = nodes.shape
    blk_count = lax.axis_size("blk")
    seq_count = lax.axis_size("seq")
    group_rows = node_dev * blk_count
    head_width = model_width // blk_count
    heads_dev = head_width // HDIM
    group_blocks, slot_count = blocks.shape
    block_rows = group_rows // group_blocks
    entries = group_blocks * slot_count
    capacity = (entries + seq_count - 1) // seq_count + 1
    score_scale = HDIM ** (-0.5)
    seq_pos = lax.axis_index("seq")
    local_perm = perm - seq_pos * group_rows
    slot_index, request = plan_requests(blocks.reshape(entries), group_blocks, seq_count, capacity)
    projected = jnp.dot(nodes, w_qkv, preferred_element_type=jnp.float32).astype(jnp.bfloat16)
    regrouped = lax.all_to_all(
        projected.reshape(node_dev, 3, blk_count, head_width),
        "blk",
        split_axis=2,
        concat_axis=0,
        tiled=True,
    )
    query_grp = regrouped[:, 0, 0]
    key_grp = regrouped[:, 1, 0]
    value_grp = regrouped[:, 2, 0]
    key_blocks = jnp.concatenate(
        [to_cluster(key_grp, local_perm), to_cluster(value_grp, local_perm)], axis=1
    )
    key_blocks = key_blocks.reshape(group_blocks, block_rows, 2 * head_width)
    wanted = lax.all_to_all(request, "seq", split_axis=0, concat_axis=0, tiled=True)
    picked = jnp.take(key_blocks, wanted, axis=0)
    fetched = lax.all_to_all(picked, "seq", split_axis=0, concat_axis=0, tiled=True)
    gathered = jnp.take(
        fetched.reshape(seq_count * capacity, block_rows, 2 * head_width), slot_index, axis=0
    )
    gathered = gathered.reshape(group_blocks, slot_count * block_rows, 2, heads_dev, HDIM)
    key_rows = gathered[:, :, 0]
    value_rows = gathered[:, :, 1]
    query_c = to_cluster(query_grp, local_perm).reshape(group_blocks, block_rows, heads_dev, HDIM)
    scores = (
        jnp.einsum("jqhd,jkhd->jhqk", query_c, key_rows, preferred_element_type=jnp.float32)
        * score_scale
    )
    row_top = jnp.max(scores, axis=-1, keepdims=True)
    raised = jnp.exp(scores - row_top)
    probs = raised / jnp.sum(raised, axis=-1, keepdims=True)
    probs_low = probs.astype(jnp.bfloat16)
    attended = jnp.einsum(
        "jhqk,jkhd->jqhd", probs_low, value_rows, preferred_element_type=jnp.float32
    ).astype(jnp.bfloat16)
    attended_grp = from_cluster(attended.reshape(group_rows, head_width), local_perm)
    mixed = lax.all_to_all(
        attended_grp.reshape(blk_count, node_dev, 1, head_width),
        "blk",
        split_axis=0,
        concat_axis=2,
        tiled=True,
    )
    mixed = mixed.reshape(node_dev, model_width)
    out = jnp.dot(mixed, w_out, preferred_element_type=jnp.float32).astype(jnp.bfloat16)
    grad_mixed = jnp.dot(grad_out, w_out.T, preferred_element_type=jnp.float32).astype(jnp.bfloat16)
    w_out_grad = lax.psum_scatter(
        lax.dot_general(
            grad_out, mixed, (((0,), (0,)), ((), ())), preferred_element_type=jnp.float32
        ),
        ("seq", "blk"),
        scatter_dimension=0,
        tiled=True,
    )
    grad_grp = lax.all_to_all(
        grad_mixed.reshape(node_dev, blk_count, head_width),
        "blk",
        split_axis=1,
        concat_axis=0,
        tiled=True,
    )[:, 0]
    grad_c = to_cluster(grad_grp, local_perm).reshape(group_blocks, block_rows, heads_dev, HDIM)
    grad_scores = jnp.einsum(
        "jqhd,jkhd->jhqk", grad_c, value_rows, preferred_element_type=jnp.float32
    )
    row_delta = jnp.sum(grad_c.astype(jnp.float32) * attended.astype(jnp.float32), axis=-1)
    row_delta = jnp.transpose(row_delta, (0, 2, 1))[..., None]
    grad_logits = (probs * (grad_scores - row_delta)).astype(jnp.bfloat16)
    grad_query = jnp.einsum(
        "jhqk,jkhd->jqhd", grad_logits, key_rows, preferred_element_type=jnp.float32
    )
    grad_query = (grad_query * score_scale).astype(jnp.bfloat16)
    key_part = jnp.einsum(
        "jhqk,jqhd->jkhd", grad_logits, query_c, preferred_element_type=jnp.float32
    )
    key_part = (key_part * score_scale).astype(jnp.bfloat16)
    value_part = jnp.einsum(
        "jhqk,jqhd->jkhd", probs_low, grad_c, preferred_element_type=jnp.float32
    ).astype(jnp.bfloat16)
    both_parts = jnp.concatenate(
        [
            key_part.reshape(entries, block_rows, head_width),
            value_part.reshape(entries, block_rows, head_width),
        ],
        axis=2,
    )
    outgoing = (
        jnp.zeros((seq_count * capacity, block_rows, 2 * head_width), jnp.bfloat16)
        .at[slot_index]
        .set(both_parts)
    )
    incoming = lax.all_to_all(
        outgoing.reshape(seq_count, capacity, block_rows, 2 * head_width),
        "seq",
        split_axis=0,
        concat_axis=0,
        tiled=True,
    )
    slot_hits = (
        wanted.reshape(seq_count * capacity)[:, None]
        == jnp.arange(group_blocks, dtype=jnp.int32)[None, :]
    ).astype(jnp.bfloat16)
    summed = jnp.einsum(
        "sb,sx->bx",
        slot_hits,
        incoming.reshape(seq_count * capacity, block_rows * 2 * head_width),
        preferred_element_type=jnp.float32,
    )
    summed = summed.astype(jnp.bfloat16).reshape(group_rows, 2 * head_width)
    stacked = jnp.stack(
        [
            grad_query.reshape(group_rows, head_width),
            summed[:, :head_width],
            summed[:, head_width:],
        ],
        axis=1,
    )
    stacked = from_cluster(stacked, local_perm)
    grad_projected = lax.all_to_all(
        stacked.reshape(blk_count, node_dev, 3, 1, head_width),
        "blk",
        split_axis=0,
        concat_axis=3,
        tiled=True,
    )
    grad_projected = grad_projected.reshape(node_dev, 3 * model_width)
    grad_nodes = jnp.dot(grad_projected, w_qkv.T, preferred_element_type=jnp.float32).astype(
        jnp.bfloat16
    )
    return (out, grad_nodes, w_out_grad)


def solution(mesh):
    placed = (P(("seq", "blk"), None), P(), P(), P("seq"), P("seq", None), P(("seq", "blk"), None))
    return jax.shard_map(
        on_device,
        mesh=mesh,
        in_specs=placed,
        out_specs=(P(("seq", "blk"), None), P(("seq", "blk"), None), P(("seq", "blk"), None)),
        check_vma=False,
    )
```

profile of v0, /device:TPU:0, one launch (start us, length us, event | category | flops | bytes accessed | tf_op | source)
XLA Modules:
  0.0 1008.5 jit_solution(2576047056582523908)
XLA Ops:
  9.1 7.4 all-to-all-start
  16.5 3.9 convolution_convert_fusion.1
  20.5 1.5 reshape.282
  22.8 2.1 copy.133
  25.6 5.3 all-to-all-start.4
  31.0 7.1 all-to-all-done.4
  38.1 3.5 all-to-all-start.1
  42.0 2.6 gather_fusion.5
  44.6 8.5 all-to-all-done.1
  53.2 2.6 gather_fusion.2
  55.8 2.6 gather_fusion.3
  58.4 1.9 gather_fusion.4
  61.7 5.4 gather_fusion
  67.1 7.5 broadcast_select_fusion
  74.5 7.8 all-to-all-start.2
  83.7 112.2 %all-to-all-done.2 = bf16[32,2,128,512]{3,2,1,0:T(8,128)(2,1)} async-done(((bf16[32,2,128,512]{3,2,1,0:T(8,128)(2,1)}), bf16[32,2,128,512]{3,2,1,0:T(8,128)(2,1)}, u32[]{:S(2)}, u32[]{:S(2)}) %all-to-all-start.2) | async-done | bytes 8388640 | tf_op jit(solution)/shard_map/all_to_all | solution.py:65
  195.9 6.1 gather_fusion.1
  202.1 13.7 %reshape.386 = bf16[4,1024,2,4,64]{4,3,2,1,0:T(4,128)(2,1)} reshape(bf16[32,128,512]{2,1,0:T(8,128)(2,1)} %gather_fusion.1) | data formatting | bytes 8388608 | tf_op jit(solution)/shard_map/jit(_take)/gather | solution.py:66
  215.8 12.8 %copy.138 = bf16[4,1024,2,4,64]{1,4,3,0,2:T(8,128)(2,1)} copy(bf16[4,1024,2,4,64]{4,3,2,1,0:T(4,128)(2,1)} %reshape.386) | data formatting | bytes 8388608 | tf_op jit(solution)/shard_map/jit(_take)/gather | solution.py:66
  228.5 2.6 broadcast_select_fusion.1
  231.1 1.9 copy-done.1
  234.4 4.2 fusion.26
  240.7 1.6 multiply_reduce_fusion.1
  242.3 2.1 convert_bitcast_fusion
  244.4 2.0 multiply_convert_fusion
  246.4 2.0 copy-done.3
  249.1 2.9 copy.151
  252.0 4.3 reshape.292
  256.3 4.5 copy.153
  260.8 4.2 reshape.293
  265.6 3.0 scatter_custom_fusion
  268.6 3.4 all-to-all-start.3
  272.0 4.5 pad_maximum_fusion
  276.5 7.6 copy.154
  284.1 4.2 broadcast_in_dim.67
  288.3 11.4 %scatter_fusion = bf16[64,128,512]{2,1,0:T(8,128)(2,1)} fusion(bf16[64,128,512]{2,1,0:T(8,128)(2,1)} %broadcast_in_dim.67, s32[32]{0:T(128)S(1)} %fusion.23, bf16[32,128,512]{2,1,0:T(8,128)(2,1)} %copy.154), kind=kCustom, calls=%fused_computation.7 | custom fusion | bytes 12583040 | tf_op jit(solution)/shard_map/scatter | solution.py:138
  299.7 15.9 %all-to-all-start.5 = ((bf16[32,2,128,512]{3,2,1,0:T(8,128)(2,1)}), bf16[32,2,128,512]{3,2,1,0:T(8,128)(2,1)}, u32[]{:S(2)}, u32[]{:S(2)}) async-start(bf16[32,2,128,512]{3,2,1,0:T(8,128)(2,1)} %bitcast.118), calls=%async_computation.5 | async-start | bytes 16777216 | tf_op jit(solution)/shard_map/all_to_all | solution.py:140
  315.9 2.6 convolution_bitcast_fusion
  318.5 5.6 copy.164
  325.4 4.4 fusion.14
  330.8 99.4 %all-to-all-done.5 = bf16[32,2,128,512]{3,2,1,0:T(8,128)(2,1)} async-done(((bf16[32,2,128,512]{3,2,1,0:T(8,128)(2,1)}), bf16[32,2,128,512]{3,2,1,0:T(8,128)(2,1)}, u32[]{:S(2)}, u32[]{:S(2)}) %all-to-all-start.5) | async-done | bytes 8388640 | tf_op jit(solution)/shard_map/all_to_all | solution.py:140
  430.2 11.8 %copy.175 = bf16[8,8,128,512]{3,1,2,0:T(8,128)(2,1)} copy(bf16[8,8,128,512]{3,2,1,0:T(8,128)(2,1)} %bitcast.55) | data formatting | bytes 16777216
  442.0 4.7 convolution_convert_fusion
  450.9 37.1 %scatter_fusion.1 = bf16[512,3,256]{2,1,0:T(4,128)(2,1)S(1)} fusion(bf16[512,3,256]{2,1,0:T(4,128)(2,1)S(1)} %broadcast_in_dim.66, s32[512]{0:T(512)S(1)} %get-tuple-element.23, bf16[512,3,256]{2,1,0:T(4,128)(2,1)} %copy.157), kind=kCustom, calls=%fused_computation.8 | custom fusion | bytes 2361344 | tf_op jit(solution)/shard_map/scatter | solution.py:30
  489.4 3.9 all-to-all-start.6
  494.5 8.5 all-to-all-done.6
  503.1 5.7 convolution_convert_fusion.2
  508.8 492.6 %reduce-scatter.4.cloned.1.call-done = f32[8,1024]{1,0:T(8,128)} async-done(((f32[1024,1024]{1,0:T(8,128)}), f32[8,1024]{1,0:T(8,128)}) %reduce-scatter.4.cloned.1.call-update) | async-done | bytes 32784
  (71 shorter events, 20.8 us)
Async XLA Ops:
  7.2 14.8 %copy-start = (bf16[1024,1024]{1,0:T(8,128)(2,1)S(1)}, bf16[1024,1024]{1,0:T(8,128)(2,1)}, u32[]{:S(2)}) copy-start(bf16[1024,1024]{1,0:T(8,128)(2,1)} %param.10) | copy-start | bytes 6291460
  9.1 16.5 %all-to-all-start = ((s32[32,1,2]{2,1,0:T(1,128)}), s32[32,1,2]{2,1,0:T(1,128)S(1)}, u32[]{:S(2)}, u32[]{:S(2)}) async-start(s32[32,1,2]{2,1,0:T(1,128)} %bitcast), calls=%async_computation | async-start | bytes 32768 | tf_op jit(solution)/shard_map/all_to_all | solution.py:63
  16.5 5.4 copy-start.4
  20.5 10.5 %copy-start.7 = (s32[512]{0:T(512)S(1)}, s32[512]{0:T(512)}, u32[]{:S(2)}) copy-start(s32[512]{0:T(512)} %param.11) | copy-start | bytes 6148
  25.6 12.4 %all-to-all-start.4 = ((bf16[128,4,256]{2,0,1:T(8,128)(2,1)}), bf16[128,4,256]{2,0,1:T(8,128)(2,1)S(1)}, u32[]{:S(2)}, u32[]{:S(2)}) async-start(bf16[128,4,256]{2,0,1:T(8,128)(2,1)} %bitcast.115), calls=%async_computation.4 | async-start | bytes 524288 | tf_op jit(solution)/shard_map/all_to_all | solution.py:103
  38.1 15.0 %all-to-all-start.1 = ((bf16[128,3,4,256]{3,0,1,2:T(8,128)(2,1)}), bf16[128,3,4,256]{3,0,1,2:T(8,128)(2,1)S(1)}, u32[]{:S(2)}, u32[]{:S(2)}) async-start(bf16[128,3,4,256]{3,0,1,2:T(8,128)(2,1)} %copy.133), calls=%async_computation.1 | async-start | bytes 1572864 | tf_op jit(solution)/shard_map/all_to_all | solution.py:49
  74.5 7.9 copy-start.6
  74.5 121.4 %all-to-all-start.2 = ((bf16[32,2,128,512]{3,2,1,0:T(8,128)(2,1)}), bf16[32,2,128,512]{3,2,1,0:T(8,128)(2,1)}, u32[]{:S(2)}, u32[]{:S(2)}) async-start(bf16[32,2,128,512]{3,2,1,0:T(8,128)(2,1)} %broadcast_select_fusion), calls=%async_computation.2 | async-start | bytes 16777216 | tf_op jit(solution)/shard_map/all_to_all | solution.py:65
  231.1 1.9 copy-start.1
  238.5 2.2 copy-start.2
  246.4 2.0 copy-start.3
  268.6 31.1 %all-to-all-start.3 = ((bf16[4,128,1,256]{3,1,2,0:T(8,128)(2,1)}), bf16[4,128,1,256]{3,1,2,0:T(8,128)(2,1)S(1)}, u32[]{:S(2)}, u32[]{:S(2)}) async-start(bf16[4,128,1,256]{3,1,2,0:T(8,128)(2,1)} %bitcast.18), calls=%async_computation.3 | async-start | bytes 524288 | tf_op jit(solution)/shard_map/all_to_all | solution.py:85
  299.7 16.2 %copy-start.5 = (bf16[128,1024]{1,0:T(8,128)(2,1)S(1)}, bf16[128,1024]{1,0:T(8,128)(2,1)}, u32[]{:S(2)}) copy-start(bf16[128,1024]{1,0:T(8,128)(2,1)} %param.13) | copy-start | bytes 786436
  299.7 130.5 %all-to-all-start.5 = ((bf16[32,2,128,512]{3,2,1,0:T(8,128)(2,1)}), bf16[32,2,128,512]{3,2,1,0:T(8,128)(2,1)}, u32[]{:S(2)}, u32[]{:S(2)}) async-start(bf16[32,2,128,512]{3,2,1,0:T(8,128)(2,1)} %bitcast.118), calls=%async_computation.5 | async-start | bytes 16777216 | tf_op jit(solution)/shard_map/all_to_all | solution.py:140
  315.6 685.7 %reduce-scatter.4.cloned.1.call-start = ((), (), s32[]{:S(2)}) async-start(), calls=%async_computation.8 | async-start | bytes 4227072
  489.4 13.6 %all-to-all-start.6 = ((bf16[4,128,3,1,256]{1,4,2,3,0:T(8,128)(2,1)}), bf16[4,128,3,1,256]{1,4,2,3,0:T(8,128)(2,1)S(1)}, u32[]{:S(2)}, u32[]{:S(2)}) async-start(bf16[4,128,3,1,256]{1,4,2,3,0:T(8,128)(2,1)} %copy.158), calls=%async_computation.6 | async-start | bytes 1572864 | tf_op jit(solution)/shard_map/all_to_all | solution.py:167
Sparse Core Ops, SparseCore 0:
  324.2 677.1 reduce-scatter.3
where the time goes:
time: 1020 us; the launch traced here: 1010 us
  waiting for transfers between devices  728 us (71%)
  local copies, waits for them, and re-layouts  164 us (16%)
  starting transfers between devices  47.3 us (5%)
  matrix products  31 us (3%)
  other arithmetic  23.4 us (2%)
  between operations  14.6 us (1%)
    unnamed x2, waiting for transfers between devices  493 us
    all_to_all x1, waiting for transfers between devices, on_device(): lax.all_to_all(picked, 'seq', split_axis=0, concat_axis=0, tiled=True)  112 us
    all_to_all x1, waiting for transfers between devices, on_device(): lax.all_to_all(outgoing.reshape(seq_count, capacity, block_rows, 2 * head...  99.4 us
    scatter x2, local copies, waits for them, and re-layouts, from_cluster(): return jnp.zeros_like(row_data).at[local_perm].set(row_data)  40.1 us
    gather x3, local copies, waits for them, and re-layouts, on_device(): jnp.take(fetched.reshape(seq_count * capacity, block_rows, 2 * head_width...  32.6 us
    unnamed x22, local copies, waits for them, and re-layouts  23.3 us
  transfers between devices with their start and end apart: 8, of which 6 were waited for; matrix products, arithmetic and copies ran while one was open for 12% of the time, Pallas kernels for 0%

commit v1 on v0

v1 whole, which is shorter than its diff:
```python
import jax
import jax.numpy as jnp
from jax import lax
from jax.experimental import pallas as pl
from jax.experimental.pallas import tpu as pltpu
from jax.sharding import PartitionSpec as P

HDIM = 64
QB = 128
GROUP = 512
SIDE = 4
BF = jnp.bfloat16
F32 = jnp.float32
MESH = pl.DeviceIdType.MESH
VMEM_BYTES = 56 * 1024 * 1024


def place():
    s = lax.axis_index("seq")
    z = lax.axis_index("blk")
    return s // 8, (s // 2) % 4, s % 2, z


def seq_of(x, y, c):
    return x * 8 + y * 2 + c


def turn(i, d):
    return lax.rem(i + (d + SIDE), SIDE)


def greet(x, y, c, z, y_steps):
    barrier = pltpu.get_barrier_semaphore()
    others = [(seq_of(x, y, c), turn(z, d)) for d in (1, 2, 3)]
    others += [(seq_of(turn(x, d), y, c), z) for d in (1, 2, 3)]
    others += [(seq_of(x, turn(y, d), c), z) for d in y_steps]
    others += [(seq_of(x, y, 1 - c), z)]
    for other in others:
        pl.semaphore_signal(barrier, inc=1, device_id=other, device_id_type=MESH)
    return lambda: pl.semaphore_wait(barrier, len(others))


def remote(src, dst, send_sem, recv_sem, device):
    return pltpu.make_async_remote_copy(
        src_ref=src,
        dst_ref=dst,
        send_sem=send_sem,
        recv_sem=recv_sem,
        device_id=device,
        device_id_type=MESH,
    )


def interleave(a, b):
    low = lax.broadcasted_iota(jnp.int32, a.shape, 1) < HDIM
    return (
        jnp.where(low, a, pltpu.roll(b, HDIM, 1)),
        jnp.where(low, pltpu.roll(a, HDIM, 1), b),
    )


def dot(a, b, ca=1, cb=0):
    return lax.dot_general(a, b, (((ca,), (cb,)), ((), ())), preferred_element_type=F32)


def store_pairs(ref, a, b):
    for half in range(2):
        cols = slice(128 * half, 128 * half + 128)
        first, second = interleave(a[:, cols], b[:, cols])
        ref[:, 256 * half : 256 * half + 128] = first.astype(BF)
        ref[:, 256 * half + 128 : 256 * half + 256] = second.astype(BF)


def gather_kernel(
    nodes, w_qkv, w_out, go, perm, blk, kv_all, qg_all, blk_all,
    wbuf, wobuf, pick, zs_kv, zr_kv, zs_qg, zr_qg, xs_kv, xs_qg,
    w_sem, zs_sem, zr_sem, xs_sem, xr_sem, ys_sem, yr_sem, cs_sem, cr_sem,
):
    x, y, c, z = place()
    group = seq_of(x, y, c)
    kv_cols = pl.ds(1024, 2048)
    load_kv = pltpu.make_async_copy(w_qkv.at[:, kv_cols], wbuf.at[:, kv_cols], w_sem.at[0])
    load_q = pltpu.make_async_copy(w_qkv.at[:, pl.ds(0, 1024)], wbuf.at[:, pl.ds(0, 1024)], w_sem.at[1])
    load_o = pltpu.make_async_copy(w_out, wobuf, w_sem.at[2])
    load_kv.start()
    load_q.start()
    load_o.start()
    ready = greet(x, y, c, z, (1, 3))

    local = perm[...] - group * GROUP
    hits = lax.broadcasted_iota(jnp.int32, (GROUP, GROUP), 0) == local
    pick[...] = jnp.where(hits, 1.0, 0.0).T.astype(BF)

    def z_copy(which, d):
        src, dst = ((zs_kv, zr_kv), (zs_qg, zr_qg))[which]
        to = turn(z, d)
        return remote(
            src.at[to], dst.at[pl.ds(pl.multiple_of(z * QB, QB), QB)],
            zs_sem.at[which, d - 1], zr_sem.at[which, d - 1], (group, to),
        )

    own_rows = pl.ds(pl.multiple_of(z * QB, QB), QB)
    load_kv.wait()
    for d in (2, 1, 3, 0):
        to = turn(z, d)
        off = pl.multiple_of(to * 256, 256)
        k = dot(nodes[...], wbuf[:, pl.ds(1024 + off, 256)])
        v = dot(nodes[...], wbuf[:, pl.ds(2048 + off, 256)])
        if d == 2:
            ready()
        if d:
            store_pairs(zs_kv.at[to], k, v)
            z_copy(0, d).start()
        else:
            store_pairs(zr_kv.at[own_rows], k, v)

    blk_copies = [
        remote(blk, blk_all.at[x], xs_sem.at[2, d - 1], xr_sem.at[2, d - 1], (seq_of(turn(x, d), y, c), z))
        for d in (1, 2, 3)
    ]
    for copy in blk_copies:
        copy.start()
    blk_all[x] = blk[...]

    load_q.wait()
    load_o.wait()
    for d in (2, 1, 3, 0):
        to = turn(z, d)
        off = pl.multiple_of(to * 256, 256)
        q = dot(nodes[...], wbuf[:, pl.ds(off, 256)])
        g = dot(go[...], wobuf[pl.ds(off, 256), :], 1, 1)
        if d:
            store_pairs(zs_qg.at[to], q, g)
            z_copy(1, d).start()
        else:
            store_pairs(zr_qg.at[own_rows], q, g)

    def to_cluster(rows, staged):
        ordered = dot(pick[...], rows[...])
        for h in range(SIDE):
            staged[h] = ordered[:, 128 * h : 128 * h + 128].astype(BF)

    def x_copy(which, d):
        to = turn(x, d)
        src = (xs_kv, xs_qg)[which].at[to]
        dst = kv_all.at[group] if which == 0 else qg_all.at[x]
        return remote(src, dst, xs_sem.at[which, d - 1], xr_sem.at[which, d - 1], (seq_of(to, y, c), z))

    def y_copy(d, k):
        mine = kv_all.at[seq_of(turn(x, -d), y, c)]
        to = seq_of(x, turn(y, (1, 3)[k]), c)
        return remote(mine, mine, ys_sem.at[d, k], yr_sem.at[d, k], (to, z))

    def pass_on(d):
        y_copy(d, 0).start()
        y_copy(d, 1).start()
        cross(d, 0).start()

    def relay(d, k):
        rows = pl.ds(256 * k, 256)
        step = (1, 3)[k]
        got = kv_all.at[seq_of(turn(x, -d), turn(y, -step), c), rows]
        return remote(got, got, ys_sem.at[d, 2 + k], yr_sem.at[d, 2 + k], (seq_of(x, turn(y, step), c), z))

    def cross(d, k):
        got = kv_all.at[seq_of(turn(x, -d), turn(y, -k), c)]
        return remote(got, got, cs_sem.at[d, k], cr_sem.at[d, k], (seq_of(x, y, 1 - c), z))

    for d in (1, 2, 3):
        z_copy(0, d).wait_recv()
    to_cluster(zr_kv, xs_kv)
    for d in (2, 1, 3):
        x_copy(0, d).start()
    kv_all[group] = xs_kv[x]
    pass_on(0)

    for d in (1, 3):
        x_copy(0, d).wait_recv()
        pass_on(d)

    for d in (1, 2, 3):
        z_copy(1, d).wait_recv()
    to_cluster(zr_qg, xs_qg)
    for d in (2, 1, 3):
        x_copy(1, d).start()
    qg_all[x] = xs_qg[x]

    x_copy(0, 2).wait_recv()
    pass_on(2)

    for d in (0, 1, 3, 2):
        for k in range(2):
            y_copy(d, k).wait_recv()
            relay(d, k).start()
            cross(d, (1, 3)[k]).start()
    for d in (0, 1, 3, 2):
        relay(d, 0).wait_recv()
        relay(d, 1).wait_recv()
        cross(d, 2).start()

    for d in (1, 2, 3):
        x_copy(1, d).wait_recv()
        blk_copies[d - 1].wait_recv()
    for d in range(SIDE):
        for k in range(SIDE):
            cross(d, k).wait_recv()
    for d in (1, 2, 3):
        for which in range(2):
            z_copy(which, d).wait_send()
            x_copy(which, d).wait_send()
        blk_copies[d - 1].wait_send()
    for d in range(SIDE):
        for k in range(2):
            y_copy(d, k).wait_send()
            relay(d, k).wait_send()
        for k in range(SIDE):
            cross(d, k).wait_send()


def attention_kernel(listed, kv_all, qg_all, dkv_all, dqa_all, keys, acc):
    acc[...] = jnp.zeros_like(acc)
    low = lax.broadcasted_iota(jnp.int32, (QB, QB), 1) < HDIM
    top = lax.broadcasted_iota(jnp.int32, (QB, QB), 0) < HDIM

    def step(j, carry):
        ids = [listed[j // 4, j % 4, t] for t in range(8)]
        for t in range(8):
            keys[t * QB : (t + 1) * QB] = kv_all[ids[t]]
        qg = qg_all[j].astype(F32)
        both = jnp.concatenate(
            [jnp.where(low, qg * HDIM ** (-0.5), 0.0), jnp.where(low, 0.0, qg)], axis=0
        ).astype(BF)
        rows = dot(keys[...], both, 1, 1)
        scores, grad_scores = rows[:, :QB], rows[:, QB:]
        raised = jnp.exp(scores - jnp.max(scores, axis=0, keepdims=True))
        probs = raised / jnp.sum(raised, axis=0, keepdims=True)
        probs_low = probs.astype(BF)
        attended = dot(keys[...], probs_low, 0, 0)
        kept = attended.astype(BF).astype(F32)
        delta = jnp.sum(jnp.where(top, 0.0, qg.T * kept), axis=0, keepdims=True)
        grad_logits = (probs * (grad_scores - delta)).astype(BF)
        grad_query = dot(keys[...], grad_logits, 0, 0) * HDIM ** (-0.5)
        dqa_all[j] = jnp.where(top, grad_query, attended).T.astype(BF)
        parts = dot(jnp.concatenate([grad_logits, probs_low], axis=1), both)
        for t in range(8):
            acc[ids[t]] += parts[t * QB : (t + 1) * QB]
        return carry

    lax.fori_loop(0, 16, step, 0)

    def finish(b, carry):
        dkv_all[b] = acc[b].astype(BF)
        return carry

    lax.fori_loop(0, 128, finish, 0)


def scatter_kernel(
    dkv, dqa, w_qkv, w_out, go, perm, out, grad_nodes, w_grad,
    wbuf, wobuf, place_hits, side, opp, y_recv, y_send, xs_kv, xr_kv, xr_qa, zs_kv, zr_kv, zs_qa, zr_qa,
    mixed, gproj, wpart, wc_send, wc_recv, wz_send, wz_recv, wx_send, wx_recv, wy_send, wy_recv,
    w_sem, zs_sem, zr_sem, xs_sem, xr_sem, ys_sem, yr_sem, cs_sem, cr_sem, ws_sem, wr_sem,
):
    x, y, c, z = place()
    group = seq_of(x, y, c)
    load_o = pltpu.make_async_copy(w_out, wobuf, w_sem.at[0])
    load_w = pltpu.make_async_copy(w_qkv, wbuf, w_sem.at[1])
    load_o.start()
    load_w.start()
    ready = greet(x, y, c, z, (1, 2, 3))
    sibling = (seq_of(x, y, 1 - c), z)

    def cross(d, k):
        xt, yt = turn(x, d), turn(y, k)
        return remote(dkv.at[seq_of(xt, yt, 1 - c)], side.at[d, k], cs_sem.at[d, k], cr_sem.at[d, k], sibling)

    def x_copy(which, d):
        to = turn(x, d)
        src = xs_kv.at[to] if which == 0 else dqa.at[to]
        dst = (xr_kv, xr_qa)[which].at[:, pl.ds(pl.multiple_of(x * 128, 128), 128)]
        return remote(src, dst, xs_sem.at[which, d - 1], xr_sem.at[which, d - 1], (seq_of(to, y, c), z))

    def z_copy(which, d):
        to = turn(z, d)
        src, dst = ((zs_kv, zr_kv), (zs_qa, zr_qa))[which]
        return remote(
            src.at[pl.ds(pl.multiple_of(to * QB, QB), QB)], dst.at[z],
            zs_sem.at[which, d - 1], zr_sem.at[which, d - 1], (group, to),
        )

    def opposite(d, k):
        step = (1, 3)[k]
        rows = pl.ds(256 * k, 256)
        return remote(
            opp.at[d, rows], opp.at[SIDE + d, rows], ys_sem.at[d, k], yr_sem.at[d, k],
            (seq_of(x, turn(y, step), c), z),
        )

    def beside(d, k):
        step = (1, 3)[k]
        return remote(
            y_send.at[d, k], y_recv.at[d, k], ys_sem.at[d, 2 + k], yr_sem.at[d, 2 + k],
            (seq_of(x, turn(y, step), c), z),
        )

    def paired(d, k):
        cross(d, k).wait_recv()
        return dkv[seq_of(turn(x, d), turn(y, k), c)].astype(F32) + side[d, k].astype(F32)

    order = (2, 1, 3, 0)
    ready()
    for k in (2, 1, 3, 0):
        for d in order:
            cross(d, k).start()
    for d in (2, 1, 3):
        x_copy(1, d).start()
    local = perm[...] - group * GROUP
    hits = lax.broadcasted_iota(jnp.int32, (GROUP, GROUP), 0) == local
    place_hits[...] = jnp.where(hits, 1.0, 0.0).astype(BF)
    own_cols = pl.ds(pl.multiple_of(x * 128, 128), 128)
    own_rows = pl.ds(pl.multiple_of(z * QB, QB), QB)

    for d in order:
        opp[d] = paired(d, 2).astype(BF)
        opposite(d, 0).start()
        opposite(d, 1).start()

    xr_qa[:, own_cols] = dqa[x]
    for d in (1, 2, 3):
        x_copy(1, d).wait_recv()
    zs_qa[...] = dot(place_hits[...], xr_qa[...]).astype(BF)
    for d in (2, 1, 3):
        z_copy(1, d).start()
    zr_qa[z] = zs_qa[own_rows]

    for d in order:
        for k in range(2):
            total = paired(d, (1, 3)[k])
            opposite(d, k).wait_recv()
            rows = slice(256 * k, 256 * k + 256)
            rest = slice(256 - 256 * k, 512 - 256 * k)
            y_send[d, k, rows] = (total[rows] + opp[SIDE + d, rows].astype(F32)).astype(BF)
            y_send[d, k, rest] = total[rest].astype(BF)
            beside(d, k).start()

    for d in (1, 2, 3):
        z_copy(1, d).wait_recv()
    for h in range(SIDE):
        for half in range(2):
            a = zr_qa[h, :, 256 * half : 256 * half + 128].astype(F32)
            b = zr_qa[h, :, 256 * half + 128 : 256 * half + 256].astype(F32)
            cols = slice(256 * h + 128 * half, 256 * h + 128 * half + 128)
            first, second = interleave(a, b)
            gproj[:, cols] = first.astype(BF)
            mixed[:, cols] = second.astype(BF)
    load_o.wait()
    out[...] = dot(mixed[...], wobuf[...]).astype(BF)
    for i in range(SIDE):
        part = dot(go[:, 256 * i : 256 * i + 256], mixed[...], 0, 0)
        wpart[4 * i : 4 * i + 4] = part.reshape(4, 2, 32, 1024)

    def w_rows(core, to):
        return wpart[:, core, pl.ds(pl.multiple_of(to * 8, 8), 8), :].reshape(QB, 1024)

    w_cross = remote(wc_send, wc_recv, ws_sem.at[0], wr_sem.at[0], sibling)
    for to in range(SIDE):
        wc_send[to] = w_rows(1 - c, to).astype(BF)
    w_cross.start()

    for d in order:
        for k in range(2):
            beside(d, k).wait_recv()
        total = paired(d, 0) + (y_recv[d, 0].astype(F32) + y_recv[d, 1].astype(F32))
        if d:
            xs_kv[turn(x, d)] = total.astype(BF)
            x_copy(0, d).start()
        else:
            xr_kv[:, own_cols] = total.astype(BF)

    def w_z(d):
        return remote(
            wz_send.at[d - 1], wz_recv.at[d - 1], ws_sem.at[d], wr_sem.at[d], (group, turn(z, d))
        )

    def w_x(d):
        return remote(
            wx_send.at[pl.ds(pl.multiple_of(turn(x, d) * 32, 32), 32)], wx_recv.at[d - 1],
            ws_sem.at[3 + d], wr_sem.at[3 + d], (seq_of(turn(x, d), y, c), z),
        )

    def w_y(d):
        return remote(
            wy_send.at[turn(y, d)], wy_recv.at[d - 1],
            ws_sem.at[6 + d], wr_sem.at[6 + d], (seq_of(x, turn(y, d), c), z),
        )

    w_cross.wait_recv()
    for d in (2, 1, 3):
        to = turn(z, d)
        wz_send[d - 1] = (w_rows(c, to) + wc_recv[to].astype(F32)).astype(BF)
        w_z(d).start()

    for d in (1, 2, 3):
        x_copy(0, d).wait_recv()
    zs_kv[...] = dot(place_hits[...], xr_kv[...]).astype(BF)
    for d in (2, 1, 3):
        z_copy(0, d).start()
    zr_kv[z] = zs_kv[own_rows]

    wsum = w_rows(c, z) + wc_recv[z].astype(F32)
    for d in (1, 2, 3):
        w_z(d).wait_recv()
        wsum += wz_recv[d - 1].astype(F32)
    wx_send[...] = wsum.astype(BF)
    for d in (2, 1, 3):
        w_x(d).start()

    for d in (1, 2, 3):
        z_copy(0, d).wait_recv()
    for h in range(SIDE):
        for half in range(2):
            a = zr_kv[h, :, 256 * half : 256 * half + 128].astype(F32)
            b = zr_kv[h, :, 256 * half + 128 : 256 * half + 256].astype(F32)
            col = 256 * h + 128 * half
            first, second = interleave(a, b)
            gproj[:, 1024 + col : 1024 + col + 128] = first.astype(BF)
            gproj[:, 2048 + col : 2048 + col + 128] = second.astype(BF)
    load_w.wait()
    for i in range(SIDE):
        rows = slice(256 * i, 256 * i + 256)
        grad_nodes[:, rows] = dot(gproj[...], wbuf[rows, :], 1, 1).astype(BF)

    wrows = wx_send[pl.ds(pl.multiple_of(x * 32, 32), 32)].astype(F32)
    for d in (1, 2, 3):
        w_x(d).wait_recv()
        wrows += wx_recv[d - 1].astype(F32)
    wy_send[...] = wrows.reshape(SIDE, 8, 1024)
    for d in (2, 1, 3):
        w_y(d).start()
    wfinal = wy_send[y]
    for d in (1, 2, 3):
        w_y(d).wait_recv()
        wfinal += wy_recv[d - 1]
    w_grad[...] = wfinal

    w_cross.wait_send()
    for d in (1, 2, 3):
        for which in range(2):
            x_copy(which, d).wait_send()
            z_copy(which, d).wait_send()
        w_z(d).wait_send()
        w_x(d).wait_send()
        w_y(d).wait_send()
    for d in range(SIDE):
        for k in range(SIDE):
            cross(d, k).wait_send()
        for k in range(2):
            opposite(d, k).wait_send()
            beside(d, k).wait_send()


def dma(*shape):
    return pltpu.SemaphoreType.DMA(shape)


def on_device(nodes, w_qkv, w_out, perm, blocks, grad_out):
    vm = pl.BlockSpec(memory_space=pltpu.VMEM)
    anywhere = pl.BlockSpec(memory_space=pl.ANY)
    sds = jax.ShapeDtypeStruct
    perm_row = perm.reshape(1, GROUP)
    blk = jnp.pad(blocks, ((0, 4), (0, 120)))
    kv_all, qg_all, blk_all = pl.pallas_call(
        gather_kernel,
        out_shape=(sds((32, GROUP, 128), BF), sds((SIDE, GROUP, 128), BF), sds((SIDE, 8, 128), jnp.int32)),
        in_specs=[vm, anywhere, anywhere, vm, vm, vm],
        out_specs=(vm, vm, vm),
        scratch_shapes=[
            pltpu.VMEM((1024, 3072), BF),
            pltpu.VMEM((1024, 1024), BF),
            pltpu.VMEM((GROUP, GROUP), BF),
            pltpu.VMEM((SIDE, QB, 512), BF),
            pltpu.VMEM((GROUP, 512), BF),
            pltpu.VMEM((SIDE, QB, 512), BF),
            pltpu.VMEM((GROUP, 512), BF),
            pltpu.VMEM((SIDE, GROUP, 128), BF),
            pltpu.VMEM((SIDE, GROUP, 128), BF),
            dma(3), dma(2, 3), dma(2, 3), dma(3, 3), dma(3, 3),
            dma(4, 4), dma(4, 4), dma(4, 4), dma(4, 4),
        ],
        compiler_params=pltpu.CompilerParams(
            collective_id=0, has_side_effects=True, vmem_limit_bytes=VMEM_BYTES
        ),
        name="gather",
    )(nodes, w_qkv, w_out, grad_out, perm_row, blk)

    dkv, dqa = pl.pallas_call(
        attention_kernel,
        out_shape=(sds((128, QB, 128), BF), sds((16, QB, 128), BF)),
        in_specs=[pl.BlockSpec(memory_space=pltpu.SMEM), vm, vm],
        out_specs=(vm, vm),
        scratch_shapes=[pltpu.VMEM((1024, 128), BF), pltpu.VMEM((128, QB, 128), F32)],
        compiler_params=pltpu.CompilerParams(vmem_limit_bytes=VMEM_BYTES),
        name="attention",
    )(blk_all, kv_all.reshape(128, QB, 128), qg_all.reshape(16, QB, 128))

    return pl.pallas_call(
        scatter_kernel,
        out_shape=(sds((QB, 1024), BF), sds((QB, 1024), BF), sds((8, 1024), F32)),
        in_specs=[vm, vm, anywhere, anywhere, vm, vm],
        out_specs=(vm, vm, vm),
        scratch_shapes=[
            pltpu.VMEM((1024, 3072), BF),
            pltpu.VMEM((1024, 1024), BF),
            pltpu.VMEM((GROUP, GROUP), BF),
            pltpu.VMEM((SIDE, SIDE, GROUP, 128), BF),
            pltpu.VMEM((2 * SIDE, GROUP, 128), BF),
            pltpu.VMEM((SIDE, 2, GROUP, 128), BF),
            pltpu.VMEM((SIDE, 2, GROUP, 128), BF),
            pltpu.VMEM((SIDE, GROUP, 128), BF),
            pltpu.VMEM((GROUP, 512), BF),
            pltpu.VMEM((GROUP, 512), BF),
            pltpu.VMEM((GROUP, 512), BF),
            pltpu.VMEM((SIDE, QB, 512), BF),
            pltpu.VMEM((GROUP, 512), BF),
            pltpu.VMEM((SIDE, QB, 512), BF),
            pltpu.VMEM((QB, 1024), BF),
            pltpu.VMEM((QB, 3072), BF),
            pltpu.VMEM((16, 2, 32, 1024), F32),
            pltpu.VMEM((SIDE, QB, 1024), BF),
            pltpu.VMEM((SIDE, QB, 1024), BF),
            pltpu.VMEM((3, QB, 1024), BF),
            pltpu.VMEM((3, QB, 1024), BF),
            pltpu.VMEM((QB, 1024), BF),
            pltpu.VMEM((3, 32, 1024), BF),
            pltpu.VMEM((SIDE, 8, 1024), F32),
            pltpu.VMEM((3, 8, 1024), F32),
            dma(2), dma(2, 3), dma(2, 3), dma(2, 3), dma(2, 3),
            dma(4, 4), dma(4, 4), dma(4, 4), dma(4, 4), dma(10), dma(10),
        ],
        compiler_params=pltpu.CompilerParams(
            collective_id=1, has_side_effects=True, vmem_limit_bytes=VMEM_BYTES
        ),
        name="scatter",
    )(dkv.reshape(32, GROUP, 128), dqa.reshape(SIDE, GROUP, 128), w_qkv, w_out, grad_out, perm_row)


def solution(mesh):
    placed = (P(("seq", "blk"), None), P(), P(), P("seq"), P("seq", None), P(("seq", "blk"), None))
    return jax.shard_map(
        on_device,
        mesh=mesh,
        in_specs=placed,
        out_specs=(P(("seq", "blk"), None), P(("seq", "blk"), None), P(("seq", "blk"), None)),
        check_vma=False,
    )
```

time: 1020 us -> 134 us (0.13); the launches traced: 1010 us -> 133 us
  waiting for transfers between devices: 728 us -> 0 us
  local copies, waits for them, and re-layouts: 164 us -> 5.99 us
  Pallas kernels: 0 us -> 126 us
  starting transfers between devices: 47.3 us -> 0 us
  matrix products: 31 us -> 0 us
  other arithmetic: 23.4 us -> 0 us
  between operations: 14.6 us -> 0.65 us
    unnamed x2 -> x0, waiting for transfers between devices: 493 us -> none
    all_to_all x7 -> x0, waiting for transfers between devices: 236 us -> none  [the longest x1 112 us: on_device(): lax.all_to_all(picked, 'seq', split_axis=0, concat_axis=0, tiled=True)]
    pallas_call x0 -> x3, Pallas kernels: none -> 126 us  [the longest x1 52.2 us: on_device(): pl.pallas_call(scatter_kernel, out_shape=(sds((QB, 1024), BF), sds((QB, 1...]
    scatter x3 -> x0, local copies, waits for them, and re-layouts: 51.5 us -> none  [the longest x2 40.1 us: from_cluster(): return jnp.zeros_like(row_data).at[local_perm].set(row_data)]
    gather x8 -> x0, local copies, waits for them, and re-layouts: 47.7 us -> none  [the longest x3 32.6 us: on_device(): jnp.take(fetched.reshape(seq_count * capacity, block_rows, 2 * head_width...]
    all_to_all x7 -> x0, starting transfers between devices: 47.3 us -> none  [the longest x1 15.9 us: on_device(): lax.all_to_all(outgoing.reshape(seq_count, capacity, block_rows, 2 * head...]
    dot_general x12 -> x0, matrix products: 31 us -> none  [the longest x1 5.74 us: on_device(): jnp.dot(grad_projected, w_qkv.T, preferred_element_type=jnp.float32)]
    unnamed x22 -> x3, local copies, waits for them, and re-layouts: 23.3 us -> 4.71 us
  transfers between devices with their start and end apart: 8 -> 0, of which waited for: 6 -> 0; matrix products, arithmetic and copies ran while one was open for 12% -> 0% of each run, Pallas kernels for 0% -> 0%
where the time goes in v1:
time: 134 us; the launch traced here: 133 us
  Pallas kernels  126 us (94%)
  local copies, waits for them, and re-layouts  5.99 us (4%)
    pallas_call x1, Pallas kernels, on_device(): pl.pallas_call(scatter_kernel, out_shape=(sds((QB, 1024), BF), sds((QB, 1...  52.2 us
    pallas_call x1, Pallas kernels, on_device(): pl.pallas_call(gather_kernel, out_shape=(sds((32, GROUP, 128), BF), sds((...  46.2 us
    pallas_call x1, Pallas kernels, on_device(): pl.pallas_call(attention_kernel, out_shape=(sds((128, QB, 128), BF), sds(...  28 us
    unnamed x3, local copies, waits for them, and re-layouts  4.71 us

profile of v1, /device:TPU:0, one launch (start us, length us, event | category | flops | bytes accessed | tf_op | source)
XLA Modules:
  0.0 133.0 jit_solution(15373041174942983207)
XLA Ops:
  0.6 1.3 pad.4.blk
  1.9 46.2 %gather.1 = (bf16[32,512,128]{2,1,0:T(8,128)(2,1)}, bf16[4,512,128]{2,1,0:T(8,128)(2,1)}, s32[4,8,128]{2,1,0:T(8,128)}) custom-call(bf16[128,1024]{1,0:T(8,128)(2,1)} %nodes.1, bf16[1024,3072]{1,0:T(8,128)(2,1)} %w_qkv.3, bf16[1024,1024]{1,0:T(8,128)(2,1)} %w_out.3, bf16[128,1024]{1,0:T(8,128)(2,1)} %go.3, s32[1,512]{1,0:T(1,128)} %bitcast.9, s32[8,128]{1,0:T(8,128)} %pad.4.blk), custom_call_target="tpu_custom_call" | custom-call | tf_op jit(solution)/shard_map/gather/pallas_call | solution.py:472
  48.1 28.0 %attention.1 = (bf16[128,128,128]{2,1,0:T(8,128)(2,1)}, bf16[16,128,128]{2,1,0:T(8,128)(2,1)}) custom-call(s32[4,8,128]{2,1,0:T(8,128)} %get-tuple-element.8.listed, bf16[128,128,128]{2,1,0:T(8,128)(2,1)} %bitcast.5, bf16[16,128,128]{2,1,0:T(8,128)(2,1)} %bitcast.8), custom_call_target="tpu_custom_call" | custom-call | tf_op jit(solution)/shard_map/attention/pallas_call | solution.py:496
  76.1 52.2 %scatter.1 = (bf16[128,1024]{1,0:T(8,128)(2,1)}, bf16[128,1024]{1,0:T(8,128)(2,1)}, f32[8,1024]{1,0:T(8,128)}) custom-call(bf16[32,512,128]{2,1,0:T(8,128)(2,1)} %bitcast.6, bf16[4,512,128]{2,1,0:T(8,128)(2,1)} %bitcast.7, bf16[1024,3072]{1,0:T(8,128)(2,1)} %w_qkv.3, bf16[1024,1024]{1,0:T(8,128)(2,1)} %w_out.3, bf16[128,1024]{1,0:T(8,128)(2,1)} %go.3, ...), custom_call_target="tpu_custom_call" | custom-call | tf_op jit(solution)/shard_map/scatter/pallas_call | solution.py:506
  128.3 1.7 %copy.12 = bf16[128,1024]{1,0:T(8,128)(2,1)} copy(bf16[128,1024]{1,0:T(8,128)(2,1)} %get-tuple-element.16) | data formatting | bytes 524288
  130.0 1.7 %copy.13 = bf16[128,1024]{1,0:T(8,128)(2,1)} copy(bf16[128,1024]{1,0:T(8,128)(2,1)} %get-tuple-element.17) | data formatting | bytes 524288
  131.7 1.4 %copy.14 = f32[8,1024]{1,0:T(8,128)} copy(f32[8,1024]{1,0:T(8,128)} %get-tuple-element.18) | data formatting | bytes 65536

commit v2 on v1

v2 whole, which is shorter than its diff:
```python
import jax
import jax.numpy as jnp
from jax import lax
from jax.experimental import pallas as pl
from jax.experimental.pallas import tpu as pltpu
from jax.sharding import PartitionSpec as P

HDIM = 64
QB = 128
GROUP = 512
SIDE = 4
BF = jnp.bfloat16
F32 = jnp.float32
MESH = pl.DeviceIdType.MESH
VMEM_BYTES = 56 * 1024 * 1024


def place():
    s = lax.axis_index("seq")
    z = lax.axis_index("blk")
    return s // 8, (s // 2) % 4, s % 2, z


def seq_of(x, y, c):
    return x * 8 + y * 2 + c


def turn(i, d):
    return lax.rem(i + (d + SIDE), SIDE)


def greet(x, y, c, z, y_steps):
    barrier = pltpu.get_barrier_semaphore()
    others = [(seq_of(x, y, c), turn(z, d)) for d in (1, 2, 3)]
    others += [(seq_of(turn(x, d), y, c), z) for d in (1, 2, 3)]
    others += [(seq_of(x, turn(y, d), c), z) for d in y_steps]
    others += [(seq_of(x, y, 1 - c), z)]
    for other in others:
        pl.semaphore_signal(barrier, inc=1, device_id=other, device_id_type=MESH)
    return lambda: pl.semaphore_wait(barrier, len(others))


def remote(src, dst, send_sem, recv_sem, device):
    return pltpu.make_async_remote_copy(
        src_ref=src,
        dst_ref=dst,
        send_sem=send_sem,
        recv_sem=recv_sem,
        device_id=device,
        device_id_type=MESH,
    )


def interleave(a, b):
    low = lax.broadcasted_iota(jnp.int32, a.shape, 1) < HDIM
    return (
        jnp.where(low, a, pltpu.roll(b, HDIM, 1)),
        jnp.where(low, pltpu.roll(a, HDIM, 1), b),
    )


def dot(a, b, ca=1, cb=0):
    return lax.dot_general(a, b, (((ca,), (cb,)), ((), ())), preferred_element_type=F32)


def store_pairs(ref, a, b):
    for half in range(2):
        cols = slice(128 * half, 128 * half + 128)
        first, second = interleave(a[:, cols], b[:, cols])
        ref[:, 256 * half : 256 * half + 128] = first.astype(BF)
        ref[:, 256 * half + 128 : 256 * half + 256] = second.astype(BF)


def gather_kernel(
    nodes, w_qkv, w_out, go, perm, blk, kv_all, qg_all, blk_all, go_all,
    wbuf, wobuf, pick, zs_kv, zr_kv, zs_qg, zr_qg, xs_kv, xs_qg,
    w_sem, zk_s, zk_r, zs_sem, zr_sem, xs_sem, xr_sem, ys_sem, yr_sem, cs_sem, cr_sem,
):
    x, y, c, z = place()
    group = seq_of(x, y, c)
    kv_cols = pl.ds(1024, 2048)
    load_kv = pltpu.make_async_copy(w_qkv.at[:, kv_cols], wbuf.at[:, kv_cols], w_sem.at[0])
    load_q = pltpu.make_async_copy(w_qkv.at[:, pl.ds(0, 1024)], wbuf.at[:, pl.ds(0, 1024)], w_sem.at[1])
    load_o = pltpu.make_async_copy(w_out, wobuf, w_sem.at[2])
    load_kv.start()
    load_q.start()
    load_o.start()
    ready = greet(x, y, c, z, (1, 3))
    own_rows = pl.ds(pl.multiple_of(z * QB, QB), QB)

    local = perm[...] - group * GROUP
    hits = lax.broadcasted_iota(jnp.int32, (GROUP, GROUP), 0) == local
    pick[...] = jnp.where(hits, 1.0, 0.0).T.astype(BF)

    def zk_copy(d, i):
        to, head = turn(z, d), turn(x, i)
        return remote(
            zs_kv.at[to, head], zr_kv.at[head, own_rows], zk_s.at[d - 1, i], zk_r.at[d - 1, i], (group, to)
        )

    def z_copy(which, d):
        to = turn(z, d)
        src = zs_qg.at[to] if which == 0 else go
        dst = (zr_qg, go_all)[which].at[own_rows]
        return remote(src, dst, zs_sem.at[which, d - 1], zr_sem.at[which, d - 1], (group, to))

    def project(first, second, put):
        for half in range(2):
            cols = slice(128 * half, 128 * half + 128)
            a, b = interleave(first[:, cols], second[:, cols])
            put(2 * half, a.astype(BF))
            put(2 * half + 1, b.astype(BF))

    load_kv.wait()
    for d in (2, 1, 3, 0):
        to = turn(z, d)
        off = pl.multiple_of(to * 256, 256)
        k = dot(nodes[...], wbuf[:, pl.ds(1024 + off, 256)])
        v = dot(nodes[...], wbuf[:, pl.ds(2048 + off, 256)])
        if d == 2:
            ready()
        if d:
            def put(h, val):
                zs_kv[to, h] = val
            project(k, v, put)
            zk_copy(d, 0).start()
        else:
            def put(h, val):
                zr_kv[h, own_rows] = val
            project(k, v, put)
    for i in (2, 1, 3):
        for d in (2, 1, 3):
            zk_copy(d, i).start()

    blk_copies = [
        remote(blk, blk_all.at[x], xs_sem.at[2, d - 1], xr_sem.at[2, d - 1], (seq_of(turn(x, d), y, c), z))
        for d in (1, 2, 3)
    ]
    for copy in blk_copies:
        copy.start()
    blk_all[x] = blk[...]

    def x_copy(which, d):
        to = turn(x, d)
        src = (xs_kv, xs_qg)[which].at[to]
        dst = kv_all.at[group] if which == 0 else qg_all.at[x]
        return remote(src, dst, xs_sem.at[which, d - 1], xr_sem.at[which, d - 1], (seq_of(to, y, c), z))

    def y_copy(d, k):
        mine = kv_all.at[seq_of(turn(x, -d), y, c)]
        to = seq_of(x, turn(y, (1, 3)[k]), c)
        return remote(mine, mine, ys_sem.at[d, k], yr_sem.at[d, k], (to, z))

    def relay(d, k):
        rows = pl.ds(256 * k, 256)
        step = (1, 3)[k]
        got = kv_all.at[seq_of(turn(x, -d), turn(y, -step), c), rows]
        return remote(got, got, ys_sem.at[d, 2 + k], yr_sem.at[d, 2 + k], (seq_of(x, turn(y, step), c), z))

    def cross(d, k):
        got = kv_all.at[seq_of(turn(x, -d), turn(y, -k), c)]
        return remote(got, got, cs_sem.at[d, k], cr_sem.at[d, k], (seq_of(x, y, 1 - c), z))

    def pass_on(d):
        y_copy(d, 0).start()
        y_copy(d, 1).start()
        cross(d, 0).start()

    load_q.wait()
    load_o.wait()
    for d in (2, 1, 3, 0):
        to = turn(z, d)
        off = pl.multiple_of(to * 256, 256)
        q = dot(nodes[...], wbuf[:, pl.ds(off, 256)])
        g = dot(go[...], wobuf[pl.ds(off, 256), :], 1, 1)
        if d:
            store_pairs(zs_qg.at[to], q, g)
        else:
            store_pairs(zr_qg.at[own_rows], q, g)
    go_all[own_rows] = go[...]

    for i in (0, 2, 1, 3):
        for d in (1, 2, 3):
            zk_copy(d, i).wait_recv()
        ordered = dot(pick[...], zr_kv[turn(x, i)]).astype(BF)
        if i:
            xs_kv[turn(x, i)] = ordered
            x_copy(0, i).start()
        else:
            kv_all[group] = ordered
            pass_on(0)
            for d in (2, 1, 3):
                z_copy(0, d).start()

    for d in (2, 1, 3):
        z_copy(1, d).start()

    x_copy(0, 2).wait_recv()
    pass_on(2)
    for d in (1, 2, 3):
        z_copy(0, d).wait_recv()
    ordered = dot(pick[...], zr_qg[...])
    for h in range(SIDE):
        xs_qg[h] = ordered[:, 128 * h : 128 * h + 128].astype(BF)
    for d in (2, 1, 3):
        x_copy(1, d).start()
    qg_all[x] = xs_qg[x]
    for d in (1, 3):
        x_copy(0, d).wait_recv()
        pass_on(d)

    for d in (0, 2, 1, 3):
        for k in range(2):
            y_copy(d, k).wait_recv()
            relay(d, k).start()
            cross(d, (1, 3)[k]).start()
    for d in (0, 2, 1, 3):
        relay(d, 0).wait_recv()
        relay(d, 1).wait_recv()
        cross(d, 2).start()

    for d in (1, 2, 3):
        x_copy(1, d).wait_recv()
        z_copy(1, d).wait_recv()
        blk_copies[d - 1].wait_recv()
    for d in range(SIDE):
        for k in range(SIDE):
            cross(d, k).wait_recv()
    for d in (1, 2, 3):
        for which in range(2):
            z_copy(which, d).wait_send()
            x_copy(which, d).wait_send()
        blk_copies[d - 1].wait_send()
        for i in range(SIDE):
            zk_copy(d, i).wait_send()
    for d in range(SIDE):
        for k in range(2):
            y_copy(d, k).wait_send()
            relay(d, k).wait_send()
        for k in range(SIDE):
            cross(d, k).wait_send()


def attention_kernel(listed, kv_all, qg_all, dkv_all, dqa_all, keys, acc):
    acc[...] = jnp.zeros_like(acc)
    low = lax.broadcasted_iota(jnp.int32, (QB, QB), 1) < HDIM
    top = lax.broadcasted_iota(jnp.int32, (QB, QB), 0) < HDIM
    scale = HDIM ** (-0.5)

    def softmax_and_grad(j, kept):
        ids = [listed[j // 4, j % 4, t] for t in range(8)]
        for t in range(8):
            kept[t * QB : (t + 1) * QB] = kv_all[ids[t]]
        qg = qg_all[j].astype(F32)
        both = jnp.concatenate([jnp.where(low, qg * scale, 0.0), jnp.where(low, 0.0, qg)], axis=0).astype(BF)
        rows = dot(kept[...], both, 1, 1)
        scores, grad_scores = rows[:, :QB], rows[:, QB:]
        raised = jnp.exp(scores - jnp.max(scores, axis=0, keepdims=True))
        probs = raised * (1.0 / jnp.sum(raised, axis=0, keepdims=True))
        delta = jnp.sum(probs * grad_scores, axis=0, keepdims=True)
        grad_logits = (probs * (grad_scores - delta)).astype(BF)
        return ids, both, jnp.concatenate([grad_logits, probs.astype(BF)], axis=1)

    def step(i, carry):
        parts_of = [softmax_and_grad(4 * i + u, keys.at[u]) for u in range(4)]
        for u, (ids, both, pair) in enumerate(parts_of):
            back = dot(keys[u], pair, 0, 0)
            dqa_all[4 * i + u] = jnp.where(top, back[:, :QB] * scale, back[:, QB:]).T.astype(BF)
            parts = dot(pair, both)
            for t in range(8):
                acc[ids[t]] += parts[t * QB : (t + 1) * QB]
        return carry

    lax.fori_loop(0, 4, step, 0)

    def finish(b, carry):
        dkv_all[b] = acc[b].astype(BF)
        return carry

    lax.fori_loop(0, 128, finish, 0, unroll=4)


def scatter_kernel(
    dkv, dqa, w_qkv, w_out, go_all, perm, out, grad_nodes, w_grad,
    wbuf, wobuf, place_hits, side, opp, y_recv, y_send, xs_kv, xr_kv, xr_qa, zs_kv, zr_kv, zs_qa, zr_qa,
    mixed, gproj, wpart, wc_send, wc_recv, wx_send, wx_recv, wy_send, wy_recv, wz_send, wz_recv,
    w_sem, zk_s, zk_r, zs_sem, zr_sem, xs_sem, xr_sem, ys_sem, yr_sem, cs_sem, cr_sem, ws_sem, wr_sem,
):
    x, y, c, z = place()
    group = seq_of(x, y, c)
    load_o = pltpu.make_async_copy(w_out, wobuf, w_sem.at[0])
    load_w = pltpu.make_async_copy(w_qkv, wbuf, w_sem.at[1])
    load_o.start()
    load_w.start()
    ready = greet(x, y, c, z, (1, 2, 3))
    sibling = (seq_of(x, y, 1 - c), z)
    own_rows = pl.ds(pl.multiple_of(z * QB, QB), QB)

    def cross(d, k):
        xt, yt = turn(x, d), turn(y, k)
        return remote(dkv.at[seq_of(xt, yt, 1 - c)], side.at[d, k], cs_sem.at[d, k], cr_sem.at[d, k], sibling)

    def x_copy(which, d):
        to = turn(x, d)
        src = xs_kv.at[to] if which == 0 else dqa.at[to]
        dst = (xr_kv, xr_qa)[which].at[x]
        return remote(src, dst, xs_sem.at[which, d - 1], xr_sem.at[which, d - 1], (seq_of(to, y, c), z))

    def zk_copy(d, i):
        to, head = turn(z, d), turn(x, i)
        rows = pl.ds(pl.multiple_of(to * QB, QB), QB)
        return remote(zs_kv.at[head, rows], zr_kv.at[z, head], zk_s.at[d - 1, i], zk_r.at[d - 1, i], (group, to))

    def zq_copy(d):
        to = turn(z, d)
        rows = pl.ds(pl.multiple_of(to * QB, QB), QB)
        return remote(zs_qa.at[rows], zr_qa.at[z], zs_sem.at[d - 1], zr_sem.at[d - 1], (group, to))

    def opposite(d, k):
        step = (1, 3)[k]
        rows = pl.ds(256 * k, 256)
        return remote(
            opp.at[d, rows], opp.at[SIDE + d, rows], ys_sem.at[d, k], yr_sem.at[d, k],
            (seq_of(x, turn(y, step), c), z),
        )

    def beside(d, k):
        step = (1, 3)[k]
        return remote(
            y_send.at[d, k], y_recv.at[d, k], ys_sem.at[d, 2 + k], yr_sem.at[d, 2 + k],
            (seq_of(x, turn(y, step), c), z),
        )

    def paired(d, k):
        cross(d, k).wait_recv()
        return dkv[seq_of(turn(x, d), turn(y, k), c)].astype(F32) + side[d, k].astype(F32)

    def to_neighbours(d):
        for k in range(2):
            total = paired(d, (1, 3)[k])
            opposite(d, k).wait_recv()
            rows = slice(256 * k, 256 * k + 256)
            rest = slice(256 - 256 * k, 512 - 256 * k)
            y_send[d, k, rows] = (total[rows] + opp[SIDE + d, rows].astype(F32)).astype(BF)
            y_send[d, k, rest] = total[rest].astype(BF)
            beside(d, k).start()

    def settle(d):
        for k in range(2):
            beside(d, k).wait_recv()
        total = paired(d, 0) + (y_recv[d, 0].astype(F32) + y_recv[d, 1].astype(F32))
        if d:
            xs_kv[turn(x, d)] = total.astype(BF)
            x_copy(0, d).start()
        else:
            xr_kv[x] = total.astype(BF)

    def w_x(d):
        return remote(
            wx_send.at[turn(x, d)], wx_recv.at[d - 1],
            ws_sem.at[d], wr_sem.at[d], (seq_of(turn(x, d), y, c), z),
        )

    def w_y(d):
        return remote(
            wy_send.at[turn(y, d)], wy_recv.at[d - 1],
            ws_sem.at[3 + d], wr_sem.at[3 + d], (seq_of(x, turn(y, d), c), z),
        )

    def w_z(d):
        return remote(
            wz_send.at[turn(z, d)], wz_recv.at[z], ws_sem.at[6 + d], wr_sem.at[6 + d], (group, turn(z, d))
        )

    order = (2, 1, 3, 0)
    ready()
    for k in (2, 1, 3, 0):
        for d in order:
            cross(d, k).start()
        if k == 2:
            for d in (2, 1, 3):
                x_copy(1, d).start()
    local = perm[...] - group * GROUP
    hits = lax.broadcasted_iota(jnp.int32, (GROUP, GROUP), 0) == local
    place_hits[...] = jnp.where(hits, 1.0, 0.0).astype(BF)
    xr_qa[x] = dqa[x]

    for d in order:
        opp[d] = paired(d, 2).astype(BF)
        opposite(d, 0).start()
        opposite(d, 1).start()
    to_neighbours(2)
    to_neighbours(1)

    for d in (1, 2, 3):
        x_copy(1, d).wait_recv()
    for h in range(SIDE):
        zs_qa[:, 128 * h : 128 * h + 128] = dot(place_hits[...], xr_qa[h]).astype(BF)
    for d in (2, 1, 3):
        zq_copy(d).start()
    zr_qa[z] = zs_qa[own_rows]
    to_neighbours(3)
    to_neighbours(0)

    group_mixed = []
    for half in range(2):
        a = zs_qa[:, 256 * half : 256 * half + 128].astype(F32)
        b = zs_qa[:, 256 * half + 128 : 256 * half + 256].astype(F32)
        group_mixed.append(interleave(a, b)[1].astype(BF))
    group_mixed = jnp.concatenate(group_mixed, axis=1)
    for i in range(SIDE):
        part = dot(go_all[:, 256 * i : 256 * i + 256], group_mixed, 0, 0)
        wpart[4 * i : 4 * i + 4] = part.reshape(4, 2, 32, 256)
    w_cross = remote(wc_send, wc_recv, ws_sem.at[0], wr_sem.at[0], sibling)
    wc_send[...] = wpart[:, 1 - c].astype(BF)
    w_cross.start()

    settle(2)

    for d in (1, 2, 3):
        zq_copy(d).wait_recv()
    for h in range(SIDE):
        for half in range(2):
            a = zr_qa[h, :, 256 * half : 256 * half + 128].astype(F32)
            b = zr_qa[h, :, 256 * half + 128 : 256 * half + 256].astype(F32)
            cols = slice(256 * h + 128 * half, 256 * h + 128 * half + 128)
            first, second = interleave(a, b)
            gproj[:, cols] = first.astype(BF)
            mixed[:, cols] = second.astype(BF)
    load_o.wait()
    out[...] = dot(mixed[...], wobuf[...]).astype(BF)

    settle(1)
    w_cross.wait_recv()
    wsum = (wpart[:, c] + wc_recv[...].astype(F32)).reshape(SIDE, QB, 256)
    wx_send[...] = wsum.astype(BF)
    for d in (2, 1, 3):
        w_x(d).start()
    settle(3)

    def settle_z(i):
        head = turn(x, i)
        if i:
            x_copy(0, SIDE - i).wait_recv()
        zs_kv[head] = dot(place_hits[...], xr_kv[head]).astype(BF)
        for d in (2, 1, 3):
            zk_copy(d, i).start()
        zr_kv[z, head] = zs_kv[head, own_rows]

    settle_z(2)
    wrows = wx_send[x].astype(F32)
    for d in (1, 2, 3):
        w_x(d).wait_recv()
        wrows += wx_recv[d - 1].astype(F32)
    wy_send[...] = wrows.reshape(SIDE, 32, 256)
    for d in (2, 1, 3):
        w_y(d).start()
    settle_z(3)
    settle(0)
    settle_z(0)
    settle_z(1)

    wrows = wy_send[y]
    for d in (1, 2, 3):
        w_y(d).wait_recv()
        wrows += wy_recv[d - 1]
    wz_send[...] = wrows.reshape(SIDE, 8, 256)
    for d in (2, 1, 3):
        w_z(d).start()
    wz_recv[z] = wz_send[z]

    for i in (2, 3, 0, 1):
        for d in (1, 2, 3):
            remote(
                zs_kv.at[turn(x, i), own_rows], zr_kv.at[turn(z, -d), turn(x, i)],
                zk_s.at[d - 1, i], zk_r.at[d - 1, i], (group, turn(z, -d)),
            ).wait_recv()
    for h in range(SIDE):
        for half in range(2):
            a = zr_kv[h, 2 * half].astype(F32)
            b = zr_kv[h, 2 * half + 1].astype(F32)
            col = 256 * h + 128 * half
            first, second = interleave(a, b)
            gproj[:, 1024 + col : 1024 + col + 128] = first.astype(BF)
            gproj[:, 2048 + col : 2048 + col + 128] = second.astype(BF)
    load_w.wait()
    for i in range(SIDE):
        rows = slice(256 * i, 256 * i + 256)
        grad_nodes[:, rows] = dot(gproj[...], wbuf[rows, :], 1, 1).astype(BF)

    for d in (1, 2, 3):
        w_z(d).wait_recv()
    for h in range(SIDE):
        w_grad[:, 256 * h : 256 * h + 256] = wz_recv[h]

    w_cross.wait_send()
    for d in (1, 2, 3):
        for which in range(2):
            x_copy(which, d).wait_send()
        zq_copy(d).wait_send()
        w_z(d).wait_send()
        w_x(d).wait_send()
        w_y(d).wait_send()
        for i in range(SIDE):
            zk_copy(d, i).wait_send()
    for d in range(SIDE):
        for k in range(SIDE):
            cross(d, k).wait_send()
        for k in range(2):
            opposite(d, k).wait_send()
            beside(d, k).wait_send()


def hand_on(*refs):
    half = len(refs) // 2
    for i in range(half):
        refs[half + i][...] = refs[i][...]


def dma(*shape):
    return pltpu.SemaphoreType.DMA(shape)


def on_device(nodes, w_qkv, w_out, perm, blocks, grad_out):
    vm = pl.BlockSpec(memory_space=pltpu.VMEM)
    anywhere = pl.BlockSpec(memory_space=pl.ANY)
    sds = jax.ShapeDtypeStruct
    perm_row = perm.reshape(1, GROUP)
    blk = jnp.pad(blocks, ((0, 4), (0, 120)))
    kv_all, qg_all, blk_all, go_all = pl.pallas_call(
        gather_kernel,
        out_shape=(
            sds((32, GROUP, 128), BF),
            sds((SIDE, GROUP, 128), BF),
            sds((SIDE, 8, 128), jnp.int32),
            sds((GROUP, 1024), BF),
        ),
        in_specs=[vm, anywhere, anywhere, vm, vm, vm],
        out_specs=(vm, vm, vm, vm),
        scratch_shapes=[
            pltpu.VMEM((1024, 3072), BF),
            pltpu.VMEM((1024, 1024), BF),
            pltpu.VMEM((GROUP, GROUP), BF),
            pltpu.VMEM((SIDE, SIDE, QB, 128), BF),
            pltpu.VMEM((SIDE, GROUP, 128), BF),
            pltpu.VMEM((SIDE, QB, 512), BF),
            pltpu.VMEM((GROUP, 512), BF),
            pltpu.VMEM((SIDE, GROUP, 128), BF),
            pltpu.VMEM((SIDE, GROUP, 128), BF),
            dma(3), dma(3, 4), dma(3, 4), dma(2, 3), dma(2, 3), dma(3, 3), dma(3, 3),
            dma(4, 4), dma(4, 4), dma(4, 4), dma(4, 4),
        ],
        compiler_params=pltpu.CompilerParams(
            collective_id=0, has_side_effects=True, vmem_limit_bytes=VMEM_BYTES
        ),
        name="gather",
    )(nodes, w_qkv, w_out, grad_out, perm_row, blk)

    dkv, dqa = pl.pallas_call(
        attention_kernel,
        out_shape=(sds((128, QB, 128), BF), sds((16, QB, 128), BF)),
        in_specs=[pl.BlockSpec(memory_space=pltpu.SMEM), vm, vm],
        out_specs=(vm, vm),
        scratch_shapes=[pltpu.VMEM((4, 1024, 128), BF), pltpu.VMEM((128, QB, 128), F32)],
        compiler_params=pltpu.CompilerParams(vmem_limit_bytes=VMEM_BYTES),
        name="attention",
    )(blk_all, kv_all.reshape(128, QB, 128), qg_all.reshape(16, QB, 128))

    shapes = (sds((QB, 1024), BF), sds((QB, 1024), BF), sds((8, 1024), F32))
    results = pl.pallas_call(
        scatter_kernel,
        out_shape=shapes,
        in_specs=[vm, vm, anywhere, anywhere, vm, vm],
        out_specs=(vm, vm, vm),
        scratch_shapes=[
            pltpu.VMEM((1024, 3072), BF),
            pltpu.VMEM((1024, 1024), BF),
            pltpu.VMEM((GROUP, GROUP), BF),
            pltpu.VMEM((SIDE, SIDE, GROUP, 128), BF),
            pltpu.VMEM((2 * SIDE, GROUP, 128), BF),
            pltpu.VMEM((SIDE, 2, GROUP, 128), BF),
            pltpu.VMEM((SIDE, 2, GROUP, 128), BF),
            pltpu.VMEM((SIDE, GROUP, 128), BF),
            pltpu.VMEM((SIDE, GROUP, 128), BF),
            pltpu.VMEM((SIDE, GROUP, 128), BF),
            pltpu.VMEM((SIDE, GROUP, 128), BF),
            pltpu.VMEM((SIDE, SIDE, QB, 128), BF),
            pltpu.VMEM((GROUP, 512), BF),
            pltpu.VMEM((SIDE, QB, 512), BF),
            pltpu.VMEM((QB, 1024), BF),
            pltpu.VMEM((QB, 3072), BF),
            pltpu.VMEM((16, 2, 32, 256), F32),
            pltpu.VMEM((16, 32, 256), BF),
            pltpu.VMEM((16, 32, 256), BF),
            pltpu.VMEM((SIDE, QB, 256), BF),
            pltpu.VMEM((3, QB, 256), BF),
            pltpu.VMEM((SIDE, 32, 256), F32),
            pltpu.VMEM((3, 32, 256), F32),
            pltpu.VMEM((SIDE, 8, 256), F32),
            pltpu.VMEM((SIDE, 8, 256), F32),
            dma(2), dma(3, 4), dma(3, 4), dma(3), dma(3), dma(2, 3), dma(2, 3),
            dma(4, 4), dma(4, 4), dma(4, 4), dma(4, 4), dma(10), dma(10),
        ],
        compiler_params=pltpu.CompilerParams(
            collective_id=1, has_side_effects=True, vmem_limit_bytes=VMEM_BYTES
        ),
        name="scatter",
    )(dkv.reshape(32, GROUP, 128), dqa.reshape(SIDE, GROUP, 128), w_qkv, w_out, go_all, perm_row)
    return pl.pallas_call(
        hand_on,
        out_shape=shapes,
        in_specs=[vm] * 3,
        out_specs=(vm,) * 3,
        name="results",
    )(*results)


def solution(mesh):
    placed = (P(("seq", "blk"), None), P(), P(), P("seq"), P("seq", None), P(("seq", "blk"), None))
    return jax.shard_map(
        on_device,
        mesh=mesh,
        in_specs=placed,
        out_specs=(P(("seq", "blk"), None), P(("seq", "blk"), None), P(("seq", "blk"), None)),
        check_vma=False,
    )
```

time: 134 us -> 102 us (0.76)
  Pallas kernels: 126 us -> 99.6 us
  local copies, waits for them, and re-layouts: 5.99 us -> 1.28 us
    pallas_call x1, Pallas kernels: 28 us -> 15.5 us  [on_device(): pl.pallas_call(attention_kernel, out_shape=(sds((128, QB, 128), BF), sds(...]
    pallas_call x1 -> x2, Pallas kernels: 52.2 us -> 42.3 us  [the longest x1 40.5 us: on_device(): pl.pallas_call(scatter_kernel, out_shape=shapes, in_specs=[vm, vm, anywhe...]
    unnamed x3 -> x0, local copies, waits for them, and re-layouts: 4.71 us -> none
    pallas_call x1, Pallas kernels: 46.2 us -> 41.7 us  [on_device(): pl.pallas_call(gather_kernel, out_shape=(sds((32, GROUP, 128), BF), sds((...]
where the time goes in v2:
time: 102 us
  Pallas kernels  99.6 us (98%)
  local copies, waits for them, and re-layouts  1.28 us (1%)
    pallas_call x1, Pallas kernels, on_device(): pl.pallas_call(gather_kernel, out_shape=(sds((32, GROUP, 128), BF), sds((...  41.7 us
    pallas_call x1, Pallas kernels, on_device(): pl.pallas_call(scatter_kernel, out_shape=shapes, in_specs=[vm, vm, anywhe...  40.5 us
    pallas_call x1, Pallas kernels, on_device(): pl.pallas_call(attention_kernel, out_shape=(sds((128, QB, 128), BF), sds(...  15.5 us

profile of v2, /device:TPU:0, one launch (start us, length us, event | category | flops | bytes accessed | tf_op | source)
XLA Modules:
  0.0 101.5 jit_solution(3787324549663306645)
XLA Ops:
  0.6 1.3 %pad.4.blk = s32[8,128]{1,0:T(8,128)} pad(s32[4,8]{1,0:T(4,128)} %param.10, s32[]{:T(128)} %constant.0.clone.1), padding=0_4x0_120 | pad | bytes 4228 | tf_op jit(solution)/shard_map/jit(_pad)/pad | solution.py:529
  1.9 41.7 %gather.1 = (bf16[32,512,128]{2,1,0:T(8,128)(2,1)}, bf16[4,512,128]{2,1,0:T(8,128)(2,1)}, s32[4,8,128]{2,1,0:T(8,128)}, bf16[512,1024]{1,0:T(8,128)(2,1)}) custom-call(bf16[128,1024]{1,0:T(8,128)(2,1)} %nodes.1, bf16[1024,3072]{1,0:T(8,128)(2,1)} %w_qkv.3, bf16[1024,1024]{1,0:T(8,128)(2,1)} %w_out.3, bf16[128,1024]{1,0:T(8,128)(2,1)} %go.1, ...), custom_call_target="tpu_custom_call" | custom-call | tf_op jit(solution)/shard_map/gather/pallas_call | solution.py:530
  43.7 15.5 %attention.1 = (bf16[128,128,128]{2,1,0:T(8,128)(2,1)}, bf16[16,128,128]{2,1,0:T(8,128)(2,1)}) custom-call(s32[4,8,128]{2,1,0:T(8,128)} %get-tuple-element.12.listed, bf16[128,128,128]{2,1,0:T(8,128)(2,1)} %bitcast.5, bf16[16,128,128]{2,1,0:T(8,128)(2,1)} %bitcast.7), custom_call_target="tpu_custom_call" | custom-call | tf_op jit(solution)/shard_map/attention/pallas_call | solution.py:559
  59.2 40.5 %scatter.1 = (bf16[128,1024]{1,0:T(8,128)(2,1)}, bf16[128,1024]{1,0:T(8,128)(2,1)}, f32[8,1024]{1,0:T(8,128)}) custom-call(bf16[32,512,128]{2,1,0:T(8,128)(2,1)} %bitcast.6, bf16[4,512,128]{2,1,0:T(8,128)(2,1)} %bitcast.8, bf16[1024,3072]{1,0:T(8,128)(2,1)} %w_qkv.3, bf16[1024,1024]{1,0:T(8,128)(2,1)} %w_out.3, bf16[512,1024]{1,0:T(8,128)(2,1)} %get-tuple-element.17.go_all, ...), custom_call_target="tpu_custom_call" | custom-call | tf_op jit(solution)/shard_map/scatter/pallas_call | solution.py:570
  99.7 1.8 %results.1 = (bf16[128,1024]{1,0:T(8,128)(2,1)}, bf16[128,1024]{1,0:T(8,128)(2,1)}, f32[8,1024]{1,0:T(8,128)}) custom-call(bf16[128,1024]{1,0:T(8,128)(2,1)} %get-tuple-element.18.refs_0_, bf16[128,1024]{1,0:T(8,128)(2,1)} %get-tuple-element.19.refs_1_, f32[8,1024]{1,0:T(8,128)} %get-tuple-element.20.refs_2_), custom_call_target="tpu_custom_call" | custom-call | tf_op jit(solution)/shard_map/results/pallas_call | solution.py:609

commit v3 on v2

v3 whole, which is shorter than its diff:
```python
import jax
import jax.numpy as jnp
from jax import lax
from jax.experimental import pallas as pl
from jax.experimental.pallas import tpu as pltpu
from jax.sharding import PartitionSpec as P

HDIM = 64
QB = 128
GROUP = 512
SIDE = 4
BF = jnp.bfloat16
F32 = jnp.float32
MESH = pl.DeviceIdType.MESH
VMEM_BYTES = 56 * 1024 * 1024


def place():
    s = lax.axis_index("seq")
    z = lax.axis_index("blk")
    return s // 8, (s // 2) % 4, s % 2, z


def seq_of(x, y, c):
    return x * 8 + y * 2 + c


def turn(i, d):
    return lax.rem(i + (d + SIDE), SIDE)


def greet(x, y, c, z, y_steps):
    barrier = pltpu.get_barrier_semaphore()
    others = [(seq_of(x, y, c), turn(z, d)) for d in (1, 2, 3)]
    others += [(seq_of(turn(x, d), y, c), z) for d in (1, 2, 3)]
    others += [(seq_of(x, turn(y, d), c), z) for d in y_steps]
    others += [(seq_of(x, y, 1 - c), z)]
    for other in others:
        pl.semaphore_signal(barrier, inc=1, device_id=other, device_id_type=MESH)
    return lambda: pl.semaphore_wait(barrier, len(others))


def remote(src, dst, send_sem, recv_sem, device):
    return pltpu.make_async_remote_copy(
        src_ref=src,
        dst_ref=dst,
        send_sem=send_sem,
        recv_sem=recv_sem,
        device_id=device,
        device_id_type=MESH,
    )


def interleave(a, b):
    low = lax.broadcasted_iota(jnp.int32, a.shape, 1) < HDIM
    return (
        jnp.where(low, a, pltpu.roll(b, HDIM, 1)),
        jnp.where(low, pltpu.roll(a, HDIM, 1), b),
    )


def dot(a, b, ca=1, cb=0):
    return lax.dot_general(a, b, (((ca,), (cb,)), ((), ())), preferred_element_type=F32)


def store_pairs(ref, a, b):
    for half in range(2):
        cols = slice(128 * half, 128 * half + 128)
        first, second = interleave(a[:, cols], b[:, cols])
        ref[:, 256 * half : 256 * half + 128] = first.astype(BF)
        ref[:, 256 * half + 128 : 256 * half + 256] = second.astype(BF)


def plan_sums(blk_all, plan):
    shape = (QB, QB)
    lane = lax.broadcasted_iota(jnp.int32, (1, QB), 1)
    flat = jnp.zeros((1, QB), jnp.int32)
    for j in range(16):
        row = jnp.where(lane < 8, blk_all[j // 4, j % 4 : j % 4 + 1, :], 0)
        flat += pltpu.roll(row, 8 * j, 1) if j else row
    down = lax.broadcasted_iota(jnp.int32, shape, 0)
    across = lax.broadcasted_iota(jnp.int32, shape, 1)
    by_lane = jnp.broadcast_to(flat, shape)
    by_row = by_lane.T

    def total(values):
        return jnp.sum(values, axis=0, keepdims=True)

    def count(hits):
        return total(jnp.where(hits, 1, 0))

    rank = count((by_row < by_lane) | ((by_row == by_lane) & (down < across)))
    hits = jnp.broadcast_to(rank, shape).T == across
    order = total(jnp.where(hits, down, 0))
    sorted_ids = total(jnp.where(hits, by_row, 0))
    goes_on = jnp.where((sorted_ids == pltpu.roll(sorted_ids, 1, 1)) & (lane > 0), 1, 0)
    last = jnp.maximum(count(by_row <= across) - 1, 0)
    some = jnp.minimum(count(by_row == across), 1)
    plan[...] = jnp.concatenate([order, goes_on, last, some, jnp.zeros((4, QB), jnp.int32)], axis=0)


def sublayer_kernel(
    nodes_in, w_qkv, w_out, go_in, perm, blk, out, grad_nodes, w_grad,
    nodes, go, wbuf, wobuf, pick, place_hits,
    zs_kv, zr_kv, zs_qg, zr_qg, xs_kv, xs_qg, kv_all, qg_all, blk_all, go_all,
    plan, plan_s, listed, keys, parts, seg, dqa,
    dkv, side, opp, y_recv, y_send, bxs_kv, bxr_kv, bxr_qa, bzs_kv, bzr_kv, bzs_qa, bzr_qa,
    mixed, gproj, wpart, wc_send, wc_recv, wx_send, wx_recv, wy_send, wy_recv, wz_send, wz_recv,
    w_sem, zk_s, zk_r, zs_sem, zr_sem, xs_sem, xr_sem, ys_sem, yr_sem, cs_sem, cr_sem,
    bzk_s, bzk_r, bzs_sem, bzr_sem, bxs_sem, bxr_sem, bys_sem, byr_sem, bcs_sem, bcr_sem, ws_sem, wr_sem,
):
    x, y, c, z = place()
    group = seq_of(x, y, c)
    sibling = (seq_of(x, y, 1 - c), z)
    order = (2, 1, 3, 0)
    kv_cols = pl.ds(1024, 2048)
    loads = [
        pltpu.make_async_copy(src, dst, w_sem.at[i])
        for i, (src, dst) in enumerate((
            (nodes_in, nodes),
            (w_qkv.at[:, kv_cols], wbuf.at[:, kv_cols]),
            (w_qkv.at[:, pl.ds(0, 1024)], wbuf.at[:, pl.ds(0, 1024)]),
            (go_in, go),
            (w_out, wobuf),
        ))
    ]
    for load in loads:
        load.start()
    ready = greet(x, y, c, z, (1, 2, 3))
    own_rows = pl.ds(pl.multiple_of(z * QB, QB), QB)

    local = perm[...] - group * GROUP
    hits = lax.broadcasted_iota(jnp.int32, (GROUP, GROUP), 0) == local
    one_hot = jnp.where(hits, 1.0, 0.0)
    pick[...] = one_hot.T.astype(BF)
    place_hits[...] = one_hot.astype(BF)

    def zk_copy(d, i):
        to, head = turn(z, d), turn(x, i)
        return remote(
            zs_kv.at[to, head], zr_kv.at[head, own_rows], zk_s.at[d - 1, i], zk_r.at[d - 1, i], (group, to)
        )

    def z_copy(which, d):
        to = turn(z, d)
        src = zs_qg.at[to] if which == 0 else go
        dst = (zr_qg, go_all)[which].at[own_rows]
        return remote(src, dst, zs_sem.at[which, d - 1], zr_sem.at[which, d - 1], (group, to))

    def project(first, second, put):
        for half in range(2):
            cols = slice(128 * half, 128 * half + 128)
            a, b = interleave(first[:, cols], second[:, cols])
            put(2 * half, a.astype(BF))
            put(2 * half + 1, b.astype(BF))

    def group_rows(g):
        return kv_all.at[pl.ds(pl.multiple_of(4 * g, 4), 4)]

    def x_copy(which, d):
        to = turn(x, d)
        src = (xs_kv, xs_qg)[which].at[to]
        dst = group_rows(group) if which == 0 else qg_all.at[x]
        return remote(src, dst, xs_sem.at[which, d - 1], xr_sem.at[which, d - 1], (seq_of(to, y, c), z))

    def y_copy(d, k):
        mine = group_rows(seq_of(turn(x, -d), y, c))
        to = seq_of(x, turn(y, (1, 3)[k]), c)
        return remote(mine, mine, ys_sem.at[d, k], yr_sem.at[d, k], (to, z))

    def relay(d, k):
        step = (1, 3)[k]
        first = pl.multiple_of(4 * seq_of(turn(x, -d), turn(y, -step), c) + 2 * k, 2)
        got = kv_all.at[pl.ds(first, 2)]
        return remote(got, got, ys_sem.at[d, 2 + k], yr_sem.at[d, 2 + k], (seq_of(x, turn(y, step), c), z))

    def cross(d, k):
        got = group_rows(seq_of(turn(x, -d), turn(y, -k), c))
        return remote(got, got, cs_sem.at[d, k], cr_sem.at[d, k], sibling)

    def pass_on(d):
        y_copy(d, 0).start()
        y_copy(d, 1).start()
        cross(d, 0).start()

    def relay_on(d):
        for k in range(2):
            y_copy(d, k).wait_recv()
            relay(d, k).start()
            cross(d, (1, 3)[k]).start()

    loads[0].wait()
    loads[1].wait()
    for d in (2, 1, 3, 0):
        to = turn(z, d)
        off = pl.multiple_of(to * 256, 256)
        k = dot(nodes[...], wbuf[:, pl.ds(1024 + off, 256)])
        v = dot(nodes[...], wbuf[:, pl.ds(2048 + off, 256)])
        if d == 2:
            ready()
        if d:
            def put(h, val):
                zs_kv[to, h] = val
            project(k, v, put)
            zk_copy(d, 0).start()
        else:
            def put(h, val):
                zr_kv[h, own_rows] = val
            project(k, v, put)
    for i in (2, 1, 3):
        for d in (2, 1, 3):
            zk_copy(d, i).start()

    blk_copies = [
        remote(blk, blk_all.at[x], xs_sem.at[2, d - 1], xr_sem.at[2, d - 1], (seq_of(turn(x, d), y, c), z))
        for d in (1, 2, 3)
    ]
    for copy in blk_copies:
        copy.start()
    blk_all[x] = blk[...]

    for load in loads[2:]:
        load.wait()
    for d in (2, 1, 3, 0):
        to = turn(z, d)
        off = pl.multiple_of(to * 256, 256)
        q = dot(nodes[...], wbuf[:, pl.ds(off, 256)])
        g = dot(go[...], wobuf[pl.ds(off, 256), :], 1, 1)
        if d:
            store_pairs(zs_qg.at[to], q, g)
        else:
            store_pairs(zr_qg.at[own_rows], q, g)
    go_all[own_rows] = go[...]

    for i in (0, 2, 1, 3):
        for d in (1, 2, 3):
            zk_copy(d, i).wait_recv()
        ordered = dot(pick[...], zr_kv[turn(x, i)]).astype(BF)
        if i:
            xs_kv[turn(x, i)] = ordered.reshape(4, QB, 128)
            x_copy(0, i).start()
        else:
            kv_all[pl.ds(pl.multiple_of(4 * group, 4), 4)] = ordered.reshape(4, QB, 128)
            pass_on(0)
            for d in (2, 1, 3):
                z_copy(0, d).start()

    relay_on(0)
    x_copy(0, 2).wait_recv()
    pass_on(2)
    for d in (1, 2, 3):
        z_copy(0, d).wait_recv()
    ordered = dot(pick[...], zr_qg[...])
    for h in range(SIDE):
        xs_qg[h] = ordered[:, 128 * h : 128 * h + 128].astype(BF)
    for d in (2, 1, 3):
        x_copy(1, d).start()
    for d in (2, 1, 3):
        z_copy(1, d).start()
    qg_all[x] = xs_qg[x]
    for d in (1, 3):
        x_copy(0, d).wait_recv()
        pass_on(d)
    relay_on(2)

    for d in (1, 2, 3):
        blk_copies[d - 1].wait_recv()
    plan_sums(blk_all, plan)
    plan_copy = pltpu.make_async_copy(plan, plan_s, w_sem.at[5])
    listed_copy = pltpu.make_async_copy(blk_all, listed, w_sem.at[6])
    plan_copy.start()
    listed_copy.start()

    relay_on(1)
    relay_on(3)
    for d in (0, 2, 1, 3):
        relay(d, 0).wait_recv()
        relay(d, 1).wait_recv()
        cross(d, 2).start()
    for d in (1, 2, 3):
        x_copy(1, d).wait_recv()
    plan_copy.wait()
    listed_copy.wait()
    for d in range(SIDE):
        for k in range(SIDE):
            cross(d, k).wait_recv()

    low = lax.broadcasted_iota(jnp.int32, (QB, QB), 1) < HDIM
    top = lax.broadcasted_iota(jnp.int32, (QB, QB), 0) < HDIM
    scale = HDIM ** (-0.5)

    def softmax_and_grad(i, u, kept):
        for t in range(8):
            kept[t * QB : (t + 1) * QB] = kv_all[listed[i, u, t]]
        qg = qg_all[i, u * QB : (u + 1) * QB].astype(F32)
        both = jnp.concatenate([jnp.where(low, qg * scale, 0.0), jnp.where(low, 0.0, qg)], axis=0).astype(BF)
        rows = dot(kept[...], both, 1, 1)
        scores, grad_scores = rows[:, :QB], rows[:, QB:]
        raised = jnp.exp(scores - jnp.max(scores, axis=0, keepdims=True))
        probs = raised * (1.0 / jnp.sum(raised, axis=0, keepdims=True))
        delta = jnp.sum(probs * grad_scores, axis=0, keepdims=True)
        grad_logits = (probs * (grad_scores - delta)).astype(BF)
        return both, jnp.concatenate([grad_logits, probs.astype(BF)], axis=1)

    def bx_qa(d):
        to = turn(x, d)
        return remote(
            dqa.at[to], bxr_qa.at[x], bxs_sem.at[1, d - 1], bxr_sem.at[1, d - 1], (seq_of(to, y, c), z)
        )

    def step(i, carry):
        pairs = [softmax_and_grad(i, u, keys.at[u]) for u in range(4)]
        for u, (both, pair) in enumerate(pairs):
            back = dot(keys[u], pair, 0, 0)
            dqa[i, u * QB : (u + 1) * QB] = jnp.where(top, back[:, :QB] * scale, back[:, QB:]).T.astype(BF)
            made = dot(pair, both).astype(BF)
            parts[pl.ds(pl.multiple_of(32 * i + 8 * u, 8), 8)] = made.reshape(8, QB, 128)
        return carry

    lax.fori_loop(0, 4, step, 0)
    for d in (2, 1, 3):
        bx_qa(d).start()
    bxr_qa[x] = dqa[x]

    def add_entry(i, run):
        run = run * plan_s[1, i].astype(F32) + parts[jnp.clip(plan_s[0, i], 0, QB - 1)].astype(F32)
        seg[i] = run
        return run

    lax.fori_loop(0, QB, add_entry, jnp.zeros((QB, 128), F32), unroll=4)

    def partial_sum(g, n):
        b = 4 * g + n
        return seg[jnp.clip(plan_s[2, b], 0, QB - 1)] * plan_s[3, b].astype(F32)

    def bcross(d, k):
        return remote(dkv.at[d, k], side.at[d, k], bcs_sem.at[d, k], bcr_sem.at[d, k], sibling)

    def bx_kv(d):
        to = turn(x, d)
        return remote(
            bxs_kv.at[to], bxr_kv.at[x], bxs_sem.at[0, d - 1], bxr_sem.at[0, d - 1], (seq_of(to, y, c), z)
        )

    def bzk_copy(d, i):
        to, head = turn(z, d), turn(x, i)
        rows = pl.ds(pl.multiple_of(to * QB, QB), QB)
        return remote(bzs_kv.at[head, rows], bzr_kv.at[z, head], bzk_s.at[d - 1, i], bzk_r.at[d - 1, i], (group, to))

    def bzq_copy(d):
        to = turn(z, d)
        rows = pl.ds(pl.multiple_of(to * QB, QB), QB)
        return remote(bzs_qa.at[rows], bzr_qa.at[z], bzs_sem.at[d - 1], bzr_sem.at[d - 1], (group, to))

    def opposite(d, k):
        half = pl.ds(2 * k, 2)
        return remote(
            opp.at[d, half], opp.at[SIDE + d, half], bys_sem.at[d, k], byr_sem.at[d, k],
            (seq_of(x, turn(y, (1, 3)[k]), c), z),
        )

    def beside(d, k):
        return remote(
            y_send.at[d, k], y_recv.at[d, k], bys_sem.at[d, 2 + k], byr_sem.at[d, 2 + k],
            (seq_of(x, turn(y, (1, 3)[k]), c), z),
        )

    def paired(d, k, n):
        return partial_sum(seq_of(turn(x, d), turn(y, k), c), n) + side[d, k, n].astype(F32)

    def to_opposite(d):
        bcross(d, 2).wait_recv()
        for n in range(4):
            opp[d, n] = paired(d, 2, n).astype(BF)
        opposite(d, 0).start()
        opposite(d, 1).start()

    def to_neighbours(d):
        for k in range(2):
            bcross(d, (1, 3)[k]).wait_recv()
            opposite(d, k).wait_recv()
            for n in range(4):
                total = paired(d, (1, 3)[k], n)
                if n // 2 == k:
                    total += opp[SIDE + d, n].astype(F32)
                y_send[d, k, n] = total.astype(BF)
            beside(d, k).start()

    def settle(d):
        bcross(d, 0).wait_recv()
        for k in range(2):
            beside(d, k).wait_recv()
        for n in range(4):
            total = paired(d, 0, n) + (y_recv[d, 0, n].astype(F32) + y_recv[d, 1, n].astype(F32))
            rows = slice(QB * n, QB * n + QB)
            if d:
                bxs_kv[turn(x, d), rows] = total.astype(BF)
            else:
                bxr_kv[x, rows] = total.astype(BF)
        if d:
            bx_kv(d).start()

    def settle_z(i):
        head = turn(x, i)
        if i:
            bx_kv(SIDE - i).wait_recv()
        bzs_kv[head] = dot(place_hits[...], bxr_kv[head]).astype(BF)
        for d in (2, 1, 3):
            bzk_copy(d, i).start()
        bzr_kv[z, head] = bzs_kv[head, own_rows]

    def w_x(d):
        return remote(
            wx_send.at[turn(x, d)], wx_recv.at[d - 1],
            ws_sem.at[d], wr_sem.at[d], (seq_of(turn(x, d), y, c), z),
        )

    def w_y(d):
        return remote(
            wy_send.at[turn(y, d)], wy_recv.at[d - 1],
            ws_sem.at[3 + d], wr_sem.at[3 + d], (seq_of(x, turn(y, d), c), z),
        )

    def w_z(d):
        return remote(
            wz_send.at[turn(z, d)], wz_recv.at[z], ws_sem.at[6 + d], wr_sem.at[6 + d], (group, turn(z, d))
        )

    for k in (2, 1, 3, 0):
        for d in order:
            for n in range(4):
                dkv[d, k, n] = partial_sum(seq_of(turn(x, d), turn(y, k), 1 - c), n).astype(BF)
            bcross(d, k).start()
    for d in order:
        to_opposite(d)
    to_neighbours(2)
    to_neighbours(1)

    for d in (1, 2, 3):
        bx_qa(d).wait_recv()
    for h in range(SIDE):
        bzs_qa[:, 128 * h : 128 * h + 128] = dot(place_hits[...], bxr_qa[h]).astype(BF)
    for d in (2, 1, 3):
        bzq_copy(d).start()
    bzr_qa[z] = bzs_qa[own_rows]
    to_neighbours(3)
    to_neighbours(0)

    for d in (1, 2, 3):
        z_copy(1, d).wait_recv()
    group_mixed = []
    for half in range(2):
        a = bzs_qa[:, 256 * half : 256 * half + 128].astype(F32)
        b = bzs_qa[:, 256 * half + 128 : 256 * half + 256].astype(F32)
        group_mixed.append(interleave(a, b)[1].astype(BF))
    group_mixed = jnp.concatenate(group_mixed, axis=1)
    for i in range(SIDE):
        part = dot(go_all[:, 256 * i : 256 * i + 256], group_mixed, 0, 0)
        wpart[4 * i : 4 * i + 4] = part.reshape(4, 2, 32, 256)
    w_cross = remote(wc_send, wc_recv, ws_sem.at[0], wr_sem.at[0], sibling)
    wc_send[...] = wpart[:, 1 - c].astype(BF)
    w_cross.start()

    settle(2)

    for d in (1, 2, 3):
        bzq_copy(d).wait_recv()
    for h in range(SIDE):
        for half in range(2):
            a = bzr_qa[h, :, 256 * half : 256 * half + 128].astype(F32)
            b = bzr_qa[h, :, 256 * half + 128 : 256 * half + 256].astype(F32)
            cols = slice(256 * h + 128 * half, 256 * h + 128 * half + 128)
            first, second = interleave(a, b)
            gproj[:, cols] = first.astype(BF)
            mixed[:, cols] = second.astype(BF)
    out[...] = dot(mixed[...], wobuf[...]).astype(BF)

    settle(1)
    w_cross.wait_recv()
    wsum = (wpart[:, c] + wc_recv[...].astype(F32)).reshape(SIDE, QB, 256)
    wx_send[...] = wsum.astype(BF)
    for d in (2, 1, 3):
        w_x(d).start()
    settle(3)

    settle_z(2)
    wrows = wx_send[x].astype(F32)
    for d in (1, 2, 3):
        w_x(d).wait_recv()
        wrows += wx_recv[d - 1].astype(F32)
    wy_send[...] = wrows.reshape(SIDE, 32, 256)
    for d in (2, 1, 3):
        w_y(d).start()
    settle_z(3)
    settle(0)
    settle_z(0)
    settle_z(1)

    wrows = wy_send[y]
    for d in (1, 2, 3):
        w_y(d).wait_recv()
        wrows += wy_recv[d - 1]
    wz_send[...] = wrows.reshape(SIDE, 8, 256)
    for d in (2, 1, 3):
        w_z(d).start()
    wz_recv[z] = wz_send[z]

    for i in (2, 3, 0, 1):
        for d in (1, 2, 3):
            remote(
                bzs_kv.at[turn(x, i), own_rows], bzr_kv.at[turn(z, -d), turn(x, i)],
                bzk_s.at[d - 1, i], bzk_r.at[d - 1, i], (group, turn(z, -d)),
            ).wait_recv()
    for h in range(SIDE):
        for half in range(2):
            a = bzr_kv[h, 2 * half].astype(F32)
            b = bzr_kv[h, 2 * half + 1].astype(F32)
            col = 256 * h + 128 * half
            first, second = interleave(a, b)
            gproj[:, 1024 + col : 1024 + col + 128] = first.astype(BF)
            gproj[:, 2048 + col : 2048 + col + 128] = second.astype(BF)
    for i in range(SIDE):
        rows = slice(256 * i, 256 * i + 256)
        grad_nodes[:, rows] = dot(gproj[...], wbuf[rows, :], 1, 1).astype(BF)

    for d in (1, 2, 3):
        w_z(d).wait_recv()
    for h in range(SIDE):
        w_grad[:, 256 * h : 256 * h + 256] = wz_recv[h]

    w_cross.wait_send()
    for d in (1, 2, 3):
        for which in range(2):
            z_copy(which, d).wait_send()
            x_copy(which, d).wait_send()
        blk_copies[d - 1].wait_send()
        bx_kv(d).wait_send()
        bx_qa(d).wait_send()
        bzq_copy(d).wait_send()
        w_z(d).wait_send()
        w_x(d).wait_send()
        w_y(d).wait_send()
        for i in range(SIDE):
            zk_copy(d, i).wait_send()
            bzk_copy(d, i).wait_send()
    for d in range(SIDE):
        for k in range(2):
            y_copy(d, k).wait_send()
            relay(d, k).wait_send()
            opposite(d, k).wait_send()
            beside(d, k).wait_send()
        for k in range(SIDE):
            cross(d, k).wait_send()
            bcross(d, k).wait_send()


def hand_on(*refs):
    half = len(refs) // 2
    for i in range(half):
        refs[half + i][...] = refs[i][...]


def dma(*shape):
    return pltpu.SemaphoreType.DMA(shape)


def low_precision(*shape):
    return pltpu.VMEM(shape, BF)


def full(*shape):
    return pltpu.VMEM(shape, F32)


def on_device(nodes, w_qkv, w_out, perm, blocks, grad_out):
    vm = pl.BlockSpec(memory_space=pltpu.VMEM)
    anywhere = pl.BlockSpec(memory_space=pl.ANY)
    sds = jax.ShapeDtypeStruct
    shapes = (sds((QB, 1024), BF), sds((QB, 1024), BF), sds((8, 1024), F32))
    low = low_precision
    heads = (SIDE, GROUP, 128)
    results = pl.pallas_call(
        sublayer_kernel,
        out_shape=shapes,
        in_specs=[anywhere, anywhere, anywhere, anywhere, vm, vm],
        out_specs=(vm, vm, vm),
        scratch_shapes=[
            low(QB, 1024), low(QB, 1024), low(1024, 3072), low(1024, 1024), low(GROUP, GROUP), low(GROUP, GROUP),
            low(SIDE, SIDE, QB, 128), low(*heads), low(SIDE, QB, 512), low(GROUP, 512),
            low(SIDE, 4, QB, 128), low(*heads), low(QB, QB, 128), low(*heads),
            pltpu.VMEM((SIDE, 8, 128), jnp.int32), low(GROUP, 1024),
            pltpu.VMEM((8, QB), jnp.int32), pltpu.SMEM((8, QB), jnp.int32), pltpu.SMEM((SIDE, 8, 128), jnp.int32),
            low(4, 1024, 128), low(QB, QB, 128), full(QB, QB, 128), low(*heads),
            low(SIDE, SIDE, 4, QB, 128), low(SIDE, SIDE, 4, QB, 128), low(2 * SIDE, 4, QB, 128),
            low(SIDE, 2, 4, QB, 128), low(SIDE, 2, 4, QB, 128),
            low(*heads), low(*heads), low(*heads), low(*heads), low(SIDE, SIDE, QB, 128),
            low(GROUP, 512), low(SIDE, QB, 512),
            low(QB, 1024), low(QB, 3072), full(16, 2, 32, 256), low(16, 32, 256), low(16, 32, 256),
            low(SIDE, QB, 256), low(3, QB, 256), full(SIDE, 32, 256), full(3, 32, 256),
            full(SIDE, 8, 256), full(SIDE, 8, 256),
            dma(7), dma(3, 4), dma(3, 4), dma(2, 3), dma(2, 3), dma(3, 3), dma(3, 3),
            dma(4, 4), dma(4, 4), dma(4, 4), dma(4, 4),
            dma(3, 4), dma(3, 4), dma(3), dma(3), dma(2, 3), dma(2, 3),
            dma(4, 4), dma(4, 4), dma(4, 4), dma(4, 4), dma(10), dma(10),
        ],
        compiler_params=pltpu.CompilerParams(
            collective_id=0, has_side_effects=True, vmem_limit_bytes=VMEM_BYTES
        ),
        name="sublayer",
    )(nodes, w_qkv, w_out, grad_out, perm.reshape(1, GROUP), jnp.pad(blocks, ((0, 4), (0, 120))))
    return pl.pallas_call(
        hand_on, out_shape=shapes, in_specs=[vm] * 3, out_specs=(vm,) * 3, name="results"
    )(*results)


def solution(mesh):
    placed = (P(("seq", "blk"), None), P(), P(), P("seq"), P("seq", None), P(("seq", "blk"), None))
    return jax.shard_map(
        on_device,
        mesh=mesh,
        in_specs=placed,
        out_specs=(P(("seq", "blk"), None), P(("seq", "blk"), None), P(("seq", "blk"), None)),
        check_vma=False,
    )
```

time: 102 us -> 85.6 us (0.84)
  Pallas kernels: 99.6 us -> 83.3 us
    pallas_call x3 -> x1, Pallas kernels: 97.8 us -> 81.5 us  [on_device(): pl.pallas_call(sublayer_kernel, out_shape=shapes, in_specs=[anywhere, any...]
where the time goes in v3:
time: 85.6 us; the launch traced here: 85.2 us
  Pallas kernels  83.3 us (97%)
  local copies, waits for them, and re-layouts  1.28 us (1%)
    pallas_call x1, Pallas kernels, on_device(): pl.pallas_call(sublayer_kernel, out_shape=shapes, in_specs=[anywhere, any...  81.5 us
    pallas_call x1, Pallas kernels, on_device(): pl.pallas_call(hand_on, out_shape=shapes, in_specs=[vm] * 3, out_specs=(v...  1.84 us

profile of v3, /device:TPU:0, one launch (start us, length us, event | category | flops | bytes accessed | tf_op | source)
XLA Modules:
  0.0 85.2 jit_solution(16775028930166223817)
XLA Ops:
  0.6 1.3 %pad.4.blk = s32[8,128]{1,0:T(8,128)} pad(s32[4,8]{1,0:T(4,128)} %param.10, s32[]{:T(128)} %constant.0.clone.1), padding=0_4x0_120 | pad | bytes 4228 | tf_op jit(solution)/shard_map/jit(_pad)/pad | solution.py:610
  1.9 81.5 %sublayer.1 = (bf16[128,1024]{1,0:T(8,128)(2,1)}, bf16[128,1024]{1,0:T(8,128)(2,1)}, f32[8,1024]{1,0:T(8,128)}) custom-call(bf16[128,1024]{1,0:T(8,128)(2,1)} %nodes_in.1, bf16[1024,3072]{1,0:T(8,128)(2,1)} %w_qkv.1, bf16[1024,1024]{1,0:T(8,128)(2,1)} %w_out.1, bf16[128,1024]{1,0:T(8,128)(2,1)} %go_in.1, s32[1,512]{1,0:T(1,128)} %bitcast.1, s32[8,128]{1,0:T(8,128)} %pad.4.blk), custom_call_target="tpu_custom_call" | custom-call | tf_op jit(solution)/shard_map/sublayer/pallas_call | solution.py:582
  83.4 1.8 %results.1 = (bf16[128,1024]{1,0:T(8,128)(2,1)}, bf16[128,1024]{1,0:T(8,128)(2,1)}, f32[8,1024]{1,0:T(8,128)}) custom-call(bf16[128,1024]{1,0:T(8,128)(2,1)} %get-tuple-element.6.refs_0_, bf16[128,1024]{1,0:T(8,128)(2,1)} %get-tuple-element.7.refs_1_, f32[8,1024]{1,0:T(8,128)} %get-tuple-element.8.refs_2_), custom_call_target="tpu_custom_call" | custom-call | tf_op jit(solution)/shard_map/results/pallas_call | solution.py:611

commit v4 on v3

--- a/solution.py
+++ b/solution.py
@@ -94,18 +94,17 @@
     order = total(jnp.where(hits, down, 0))
     sorted_ids = total(jnp.where(hits, by_row, 0))
     goes_on = jnp.where((sorted_ids == pltpu.roll(sorted_ids, 1, 1)) & (lane > 0), 1, 0)
-    last = jnp.maximum(count(by_row <= across) - 1, 0)
-    some = jnp.minimum(count(by_row == across), 1)
-    plan[...] = jnp.concatenate([order, goes_on, last, some, jnp.zeros((4, QB), jnp.int32)], axis=0)
+    last = jnp.where(count(by_row == across) > 0, count(by_row <= across) - 1, QB)
+    plan[...] = jnp.concatenate([order, goes_on, last, jnp.zeros((5, QB), jnp.int32)], axis=0)
 
 
 def sublayer_kernel(
     nodes_in, w_qkv, w_out, go_in, perm, blk, out, grad_nodes, w_grad,
     nodes, go, wbuf, wobuf, pick, place_hits,
     zs_kv, zr_kv, zs_qg, zr_qg, xs_kv, xs_qg, kv_all, qg_all, blk_all, go_all,
-    plan, plan_s, listed, keys, parts, seg, dqa,
+    blk_pad, plan, plan_s, listed, keys, parts, seg, dqa,
     dkv, side, opp, y_recv, y_send, bxs_kv, bxr_kv, bxr_qa, bzs_kv, bzr_kv, bzs_qa, bzr_qa,
-    mixed, gproj, wpart, wc_send, wc_recv, wx_send, wx_recv, wy_send, wy_recv, wz_send, wz_recv,
+    mixed, gproj, gacc, wpart, wc_send, wc_recv, wx_send, wx_recv, wy_send, wy_recv, wz_send, wz_recv,
     w_sem, zk_s, zk_r, zs_sem, zr_sem, xs_sem, xr_sem, ys_sem, yr_sem, cs_sem, cr_sem,
     bzk_s, bzk_r, bzs_sem, bzr_sem, bxs_sem, bxr_sem, bys_sem, byr_sem, bcs_sem, bcr_sem, ws_sem, wr_sem,
 ):
@@ -129,12 +128,6 @@
     ready = greet(x, y, c, z, (1, 2, 3))
     own_rows = pl.ds(pl.multiple_of(z * QB, QB), QB)
 
-    local = perm[...] - group * GROUP
-    hits = lax.broadcasted_iota(jnp.int32, (GROUP, GROUP), 0) == local
-    one_hot = jnp.where(hits, 1.0, 0.0)
-    pick[...] = one_hot.T.astype(BF)
-    place_hits[...] = one_hot.astype(BF)
-
     def zk_copy(d, i):
         to, head = turn(z, d), turn(x, i)
         return remote(
@@ -207,17 +200,25 @@
             def put(h, val):
                 zr_kv[h, own_rows] = val
             project(k, v, put)
-    for i in (2, 1, 3):
+    for i in (1, 3, 2):
         for d in (2, 1, 3):
             zk_copy(d, i).start()
 
+    local = perm[...] - group * GROUP
+    hits = lax.broadcasted_iota(jnp.int32, (GROUP, GROUP), 0) == local
+    one_hot = jnp.where(hits, 1.0, 0.0)
+    pick[...] = one_hot.T.astype(BF)
+    place_hits[...] = one_hot.astype(BF)
+
+    blk_pad[...] = jnp.zeros_like(blk_pad)
+    blk_pad[0:4, 0:8] = blk[...]
     blk_copies = [
-        remote(blk, blk_all.at[x], xs_sem.at[2, d - 1], xr_sem.at[2, d - 1], (seq_of(turn(x, d), y, c), z))
+        remote(blk_pad, blk_all.at[x], xs_sem.at[2, d - 1], xr_sem.at[2, d - 1], (seq_of(turn(x, d), y, c), z))
         for d in (1, 2, 3)
     ]
     for copy in blk_copies:
         copy.start()
-    blk_all[x] = blk[...]
+    blk_all[x] = blk_pad[...]
 
     for load in loads[2:]:
         load.wait()
@@ -232,7 +233,7 @@
             store_pairs(zr_qg.at[own_rows], q, g)
     go_all[own_rows] = go[...]
 
-    for i in (0, 2, 1, 3):
+    for i in (0, 1, 3, 2):
         for d in (1, 2, 3):
             zk_copy(d, i).wait_recv()
         ordered = dot(pick[...], zr_kv[turn(x, i)]).astype(BF)
@@ -246,8 +247,10 @@
                 z_copy(0, d).start()
 
     relay_on(0)
-    x_copy(0, 2).wait_recv()
-    pass_on(2)
+    for d in (1, 3, 2):
+        x_copy(0, d).wait_recv()
+        pass_on(d)
+    relay_on(1)
     for d in (1, 2, 3):
         z_copy(0, d).wait_recv()
     ordered = dot(pick[...], zr_qg[...])
@@ -258,10 +261,7 @@
     for d in (2, 1, 3):
         z_copy(1, d).start()
     qg_all[x] = xs_qg[x]
-    for d in (1, 3):
-        x_copy(0, d).wait_recv()
-        pass_on(d)
-    relay_on(2)
+    relay_on(3)
 
     for d in (1, 2, 3):
         blk_copies[d - 1].wait_recv()
@@ -271,9 +271,8 @@
     plan_copy.start()
     listed_copy.start()
 
-    relay_on(1)
-    relay_on(3)
-    for d in (0, 2, 1, 3):
+    relay_on(2)
+    for d in (0, 1, 3, 2):
         relay(d, 0).wait_recv()
         relay(d, 1).wait_recv()
         cross(d, 2).start()
@@ -327,11 +326,12 @@
         seg[i] = run
         return run
 
+    seg[QB] = jnp.zeros((QB, 128), F32)
     lax.fori_loop(0, QB, add_entry, jnp.zeros((QB, 128), F32), unroll=4)
 
     def partial_sum(g, n):
         b = 4 * g + n
-        return seg[jnp.clip(plan_s[2, b], 0, QB - 1)] * plan_s[3, b].astype(F32)
+        return seg[jnp.clip(plan_s[2, b], 0, QB)]
 
     def bcross(d, k):
         return remote(dkv.at[d, k], side.at[d, k], bcs_sem.at[d, k], bcr_sem.at[d, k], sibling)
@@ -433,8 +433,8 @@
             bcross(d, k).start()
     for d in order:
         to_opposite(d)
-    to_neighbours(2)
-    to_neighbours(1)
+    for d in order:
+        to_neighbours(d)
 
     for d in (1, 2, 3):
         bx_qa(d).wait_recv()
@@ -443,8 +443,6 @@
     for d in (2, 1, 3):
         bzq_copy(d).start()
     bzr_qa[z] = bzs_qa[own_rows]
-    to_neighbours(3)
-    to_neighbours(0)
 
     for d in (1, 2, 3):
         z_copy(1, d).wait_recv()
@@ -461,7 +459,45 @@
     wc_send[...] = wpart[:, 1 - c].astype(BF)
     w_cross.start()
 
+    for d in (1, 2, 3):
+        x_copy(0, d).wait_send()
+        x_copy(1, d).wait_send()
+        z_copy(0, d).wait_send()
+        z_copy(1, d).wait_send()
+        bx_qa(d).wait_send()
+        blk_copies[d - 1].wait_send()
+        for i in range(SIDE):
+            zk_copy(d, i).wait_send()
+    for d in range(SIDE):
+        for k in range(2):
+            y_copy(d, k).wait_send()
+            relay(d, k).wait_send()
+            opposite(d, k).wait_send()
+        for k in range(SIDE):
+            cross(d, k).wait_send()
+            bcross(d, k).wait_send()
+
     settle(2)
+    settle(1)
+    w_cross.wait_recv()
+    wsum = (wpart[:, c] + wc_recv[...].astype(F32)).reshape(SIDE, QB, 256)
+    wx_send[...] = wsum.astype(BF)
+    for d in (2, 1, 3):
+        w_x(d).start()
+    settle(3)
+    settle_z(2)
+    settle(0)
+    settle_z(0)
+    settle_z(3)
+    settle_z(1)
+
+    wrows = wx_send[x].astype(F32)
+    for d in (1, 2, 3):
+        w_x(d).wait_recv()
+        wrows += wx_recv[d - 1].astype(F32)
+    wy_send[...] = wrows.reshape(SIDE, 32, 256)
+    for d in (2, 1, 3):
+        w_y(d).start()
 
     for d in (1, 2, 3):
         bzq_copy(d).wait_recv()
@@ -474,27 +510,9 @@
             gproj[:, cols] = first.astype(BF)
             mixed[:, cols] = second.astype(BF)
     out[...] = dot(mixed[...], wobuf[...]).astype(BF)
-
-    settle(1)
-    w_cross.wait_recv()
-    wsum = (wpart[:, c] + wc_recv[...].astype(F32)).reshape(SIDE, QB, 256)
-    wx_send[...] = wsum.astype(BF)
-    for d in (2, 1, 3):
-        w_x(d).start()
-    settle(3)
-
-    settle_z(2)
-    wrows = wx_send[x].astype(F32)
-    for d in (1, 2, 3):
-        w_x(d).wait_recv()
-        wrows += wx_recv[d - 1].astype(F32)
-    wy_send[...] = wrows.reshape(SIDE, 32, 256)
-    for d in (2, 1, 3):
-        w_y(d).start()
-    settle_z(3)
-    settle(0)
-    settle_z(0)
-    settle_z(1)
+    for i in range(SIDE):
+        rows = slice(256 * i, 256 * i + 256)
+        gacc[:, rows] = dot(gproj[:, :1024], wbuf[rows, :1024], 1, 1)
 
     wrows = wy_send[y]
     for d in (1, 2, 3):
@@ -505,12 +523,9 @@
         w_z(d).start()
     wz_recv[z] = wz_send[z]
 
-    for i in (2, 3, 0, 1):
+    for i in range(SIDE):
         for d in (1, 2, 3):
-            remote(
-                bzs_kv.at[turn(x, i), own_rows], bzr_kv.at[turn(z, -d), turn(x, i)],
-                bzk_s.at[d - 1, i], bzk_r.at[d - 1, i], (group, turn(z, -d)),
-            ).wait_recv()
+            bzk_copy(d, i).wait_recv()
     for h in range(SIDE):
         for half in range(2):
             a = bzr_kv[h, 2 * half].astype(F32)
@@ -521,7 +536,7 @@
             gproj[:, 2048 + col : 2048 + col + 128] = second.astype(BF)
     for i in range(SIDE):
         rows = slice(256 * i, 256 * i + 256)
-        grad_nodes[:, rows] = dot(gproj[...], wbuf[rows, :], 1, 1).astype(BF)
+        grad_nodes[:, rows] = (gacc[:, rows] + dot(gproj[:, 1024:], wbuf[rows, 1024:], 1, 1)).astype(BF)
 
     for d in (1, 2, 3):
         w_z(d).wait_recv()
@@ -530,28 +545,16 @@
 
     w_cross.wait_send()
     for d in (1, 2, 3):
-        for which in range(2):
-            z_copy(which, d).wait_send()
-            x_copy(which, d).wait_send()
-        blk_copies[d - 1].wait_send()
         bx_kv(d).wait_send()
-        bx_qa(d).wait_send()
         bzq_copy(d).wait_send()
         w_z(d).wait_send()
         w_x(d).wait_send()
         w_y(d).wait_send()
         for i in range(SIDE):
-            zk_copy(d, i).wait_send()
             bzk_copy(d, i).wait_send()
     for d in range(SIDE):
         for k in range(2):
-            y_copy(d, k).wait_send()
-            relay(d, k).wait_send()
-            opposite(d, k).wait_send()
             beside(d, k).wait_send()
-        for k in range(SIDE):
-            cross(d, k).wait_send()
-            bcross(d, k).wait_send()
 
 
 def hand_on(*refs):
@@ -589,13 +592,13 @@
             low(SIDE, SIDE, QB, 128), low(*heads), low(SIDE, QB, 512), low(GROUP, 512),
             low(SIDE, 4, QB, 128), low(*heads), low(QB, QB, 128), low(*heads),
             pltpu.VMEM((SIDE, 8, 128), jnp.int32), low(GROUP, 1024),
-            pltpu.VMEM((8, QB), jnp.int32), pltpu.SMEM((8, QB), jnp.int32), pltpu.SMEM((SIDE, 8, 128), jnp.int32),
-            low(4, 1024, 128), low(QB, QB, 128), full(QB, QB, 128), low(*heads),
+            pltpu.VMEM((8, QB), jnp.int32), pltpu.VMEM((8, QB), jnp.int32), pltpu.SMEM((8, QB), jnp.int32), pltpu.SMEM((SIDE, 8, 128), jnp.int32),
+            low(4, 1024, 128), low(QB, QB, 128), full(QB + 1, QB, 128), low(*heads),
             low(SIDE, SIDE, 4, QB, 128), low(SIDE, SIDE, 4, QB, 128), low(2 * SIDE, 4, QB, 128),
             low(SIDE, 2, 4, QB, 128), low(SIDE, 2, 4, QB, 128),
             low(*heads), low(*heads), low(*heads), low(*heads), low(SIDE, SIDE, QB, 128),
             low(GROUP, 512), low(SIDE, QB, 512),
-            low(QB, 1024), low(QB, 3072), full(16, 2, 32, 256), low(16, 32, 256), low(16, 32, 256),
+            low(QB, 1024), low(QB, 3072), full(QB, 1024), full(16, 2, 32, 256), low(16, 32, 256), low(16, 32, 256),
             low(SIDE, QB, 256), low(3, QB, 256), full(SIDE, 32, 256), full(3, 32, 256),
             full(SIDE, 8, 256), full(SIDE, 8, 256),
             dma(7), dma(3, 4), dma(3, 4), dma(2, 3), dma(2, 3), dma(3, 3), dma(3, 3),
@@ -607,7 +610,7 @@
             collective_id=0, has_side_effects=True, vmem_limit_bytes=VMEM_BYTES
         ),
         name="sublayer",
-    )(nodes, w_qkv, w_out, grad_out, perm.reshape(1, GROUP), jnp.pad(blocks, ((0, 4), (0, 120))))
+    )(nodes, w_qkv, w_out, grad_out, perm.reshape(1, GROUP), blocks)
     return pl.pallas_call(
         hand_on, out_shape=shapes, in_specs=[vm] * 3, out_specs=(vm,) * 3, name="results"
     )(*results)

time: 85.6 us -> 81.8 us (0.956)
  Pallas kernels: 83.3 us -> 81 us
  local copies, waits for them, and re-layouts: 1.28 us -> 0 us
    pallas_call x1, Pallas kernels: 81.5 us -> 79.1 us  [on_device(): pl.pallas_call(sublayer_kernel, out_shape=shapes, in_specs=[anywhere, any...]
    pad x1 -> x0, local copies, waits for them, and re-layouts: 1.28 us -> none  [on_device(): jnp.pad(blocks, ((0, 4), (0, 120)))]
where the time goes in v4:
time: 81.8 us; the launch traced here: 81.6 us
  Pallas kernels  81 us (99%)
    pallas_call x1, Pallas kernels, on_device(): pl.pallas_call(sublayer_kernel, out_shape=shapes, in_specs=[anywhere, any...  79.1 us
    pallas_call x1, Pallas kernels, on_device(): pl.pallas_call(hand_on, out_shape=shapes, in_specs=[vm] * 3, out_specs=(v...  1.84 us

profile of v4, /device:TPU:0, one launch (start us, length us, event | category | flops | bytes accessed | tf_op | source)
XLA Modules:
  0.0 81.6 jit_solution(1357255151997109013)
XLA Ops:
  0.6 79.1 %sublayer.1 = (bf16[128,1024]{1,0:T(8,128)(2,1)}, bf16[128,1024]{1,0:T(8,128)(2,1)}, f32[8,1024]{1,0:T(8,128)}) custom-call(bf16[128,1024]{1,0:T(8,128)(2,1)} %nodes_in.1, bf16[1024,3072]{1,0:T(8,128)(2,1)} %w_qkv.1, bf16[1024,1024]{1,0:T(8,128)(2,1)} %w_out.1, bf16[128,1024]{1,0:T(8,128)(2,1)} %go_in.1, s32[1,512]{1,0:T(1,128)} %bitcast.1, s32[4,8]{1,0:T(4,128)} %blk.1), custom_call_target="tpu_custom_call" | custom-call | tf_op jit(solution)/shard_map/sublayer/pallas_call | solution.py:585
  79.8 1.8 %results.1 = (bf16[128,1024]{1,0:T(8,128)(2,1)}, bf16[128,1024]{1,0:T(8,128)(2,1)}, f32[8,1024]{1,0:T(8,128)}) custom-call(bf16[128,1024]{1,0:T(8,128)(2,1)} %get-tuple-element.6.refs_0_, bf16[128,1024]{1,0:T(8,128)(2,1)} %get-tuple-element.7.refs_1_, f32[8,1024]{1,0:T(8,128)} %get-tuple-element.8.refs_2_), custom_call_target="tpu_custom_call" | custom-call | tf_op jit(solution)/shard_map/results/pallas_call | solution.py:614

commit v5 on v4

--- a/solution.py
+++ b/solution.py
@@ -105,8 +105,8 @@
     blk_pad, plan, plan_s, listed, keys, parts, seg, dqa,
     dkv, side, opp, y_recv, y_send, bxs_kv, bxr_kv, bxr_qa, bzs_kv, bzr_kv, bzs_qa, bzr_qa,
     mixed, gproj, gacc, wpart, wc_send, wc_recv, wx_send, wx_recv, wy_send, wy_recv, wz_send, wz_recv,
-    w_sem, zk_s, zk_r, zs_sem, zr_sem, xs_sem, xr_sem, ys_sem, yr_sem, cs_sem, cr_sem,
-    bzk_s, bzk_r, bzs_sem, bzr_sem, bxs_sem, bxr_sem, bys_sem, byr_sem, bcs_sem, bcr_sem, ws_sem, wr_sem,
+    w_sem, send, zk_r, zr_sem, xr_sem, yr_sem, rr_sem, cr_sem,
+    bzr_sem, bxr_sem, byr_sem, bcr_sem, wr_sem,
 ):
     x, y, c, z = place()
     group = seq_of(x, y, c)
@@ -128,17 +128,24 @@
     ready = greet(x, y, c, z, (1, 2, 3))
     own_rows = pl.ds(pl.multiple_of(z * QB, QB), QB)
 
+    def arrived(ref, sem):
+        remote(ref, ref, send.at[0], sem, sibling).wait_recv()
+
+    def sent(blocks, i):
+        ref = kv_all.at[pl.ds(0, blocks)]
+        remote(ref, ref, send.at[i], cr_sem.at[0], sibling).wait_send()
+
     def zk_copy(d, i):
         to, head = turn(z, d), turn(x, i)
         return remote(
-            zs_kv.at[to, head], zr_kv.at[head, own_rows], zk_s.at[d - 1, i], zk_r.at[d - 1, i], (group, to)
+            zs_kv.at[to, head], zr_kv.at[head, own_rows], send.at[0], zk_r.at[i], (group, to)
         )
 
     def z_copy(which, d):
         to = turn(z, d)
         src = zs_qg.at[to] if which == 0 else go
         dst = (zr_qg, go_all)[which].at[own_rows]
-        return remote(src, dst, zs_sem.at[which, d - 1], zr_sem.at[which, d - 1], (group, to))
+        return remote(src, dst, send.at[0], zr_sem.at[which], (group, to))
 
     def project(first, second, put):
         for half in range(2):
@@ -154,32 +161,38 @@
         to = turn(x, d)
         src = (xs_kv, xs_qg)[which].at[to]
         dst = group_rows(group) if which == 0 else qg_all.at[x]
-        return remote(src, dst, xs_sem.at[which, d - 1], xr_sem.at[which, d - 1], (seq_of(to, y, c), z))
-
-    def y_copy(d, k):
-        mine = group_rows(seq_of(turn(x, -d), y, c))
+        sem = xr_sem.at[d - 1] if which == 0 else xr_sem.at[3]
+        return remote(src, dst, send.at[1 - which], sem, (seq_of(to, y, c), z))
+
+    def y_copy(d, k, h):
+        half = k if h == 0 else 1 - k
+        first = pl.multiple_of(4 * seq_of(turn(x, -d), y, c) + 2 * half, 2)
+        mine = kv_all.at[pl.ds(first, 2)]
         to = seq_of(x, turn(y, (1, 3)[k]), c)
-        return remote(mine, mine, ys_sem.at[d, k], yr_sem.at[d, k], (to, z))
+        return remote(mine, mine, send.at[1], yr_sem.at[d, k, h], (to, z))
 
     def relay(d, k):
         step = (1, 3)[k]
         first = pl.multiple_of(4 * seq_of(turn(x, -d), turn(y, -step), c) + 2 * k, 2)
         got = kv_all.at[pl.ds(first, 2)]
-        return remote(got, got, ys_sem.at[d, 2 + k], yr_sem.at[d, 2 + k], (seq_of(x, turn(y, step), c), z))
+        return remote(got, got, send.at[1], rr_sem.at[d], (seq_of(x, turn(y, step), c), z))
 
     def cross(d, k):
         got = group_rows(seq_of(turn(x, -d), turn(y, -k), c))
-        return remote(got, got, cs_sem.at[d, k], cr_sem.at[d, k], sibling)
+        return remote(got, got, send.at[1], cr_sem.at[0], sibling)
 
     def pass_on(d):
-        y_copy(d, 0).start()
-        y_copy(d, 1).start()
+        for h in range(2):
+            for k in range(2):
+                y_copy(d, k, h).start()
         cross(d, 0).start()
 
     def relay_on(d):
         for k in range(2):
-            y_copy(d, k).wait_recv()
+            y_copy(d, k, 0).wait_recv()
             relay(d, k).start()
+        for k in range(2):
+            y_copy(d, k, 1).wait_recv()
             cross(d, (1, 3)[k]).start()
 
     loads[0].wait()
@@ -213,7 +226,7 @@
     blk_pad[...] = jnp.zeros_like(blk_pad)
     blk_pad[0:4, 0:8] = blk[...]
     blk_copies = [
-        remote(blk_pad, blk_all.at[x], xs_sem.at[2, d - 1], xr_sem.at[2, d - 1], (seq_of(turn(x, d), y, c), z))
+        remote(blk_pad, blk_all.at[x], send.at[2], xr_sem.at[4], (seq_of(turn(x, d), y, c), z))
         for d in (1, 2, 3)
     ]
     for copy in blk_copies:
@@ -234,8 +247,7 @@
     go_all[own_rows] = go[...]
 
     for i in (0, 1, 3, 2):
-        for d in (1, 2, 3):
-            zk_copy(d, i).wait_recv()
+        arrived(zr_kv.at[0, pl.ds(0, 3 * QB)], zk_r.at[i])
         ordered = dot(pick[...], zr_kv[turn(x, i)]).astype(BF)
         if i:
             xs_kv[turn(x, i)] = ordered.reshape(4, QB, 128)
@@ -251,8 +263,7 @@
         x_copy(0, d).wait_recv()
         pass_on(d)
     relay_on(1)
-    for d in (1, 2, 3):
-        z_copy(0, d).wait_recv()
+    arrived(zr_qg.at[pl.ds(0, 3 * QB)], zr_sem.at[0])
     ordered = dot(pick[...], zr_qg[...])
     for h in range(SIDE):
         xs_qg[h] = ordered[:, 128 * h : 128 * h + 128].astype(BF)
@@ -263,8 +274,7 @@
     qg_all[x] = xs_qg[x]
     relay_on(3)
 
-    for d in (1, 2, 3):
-        blk_copies[d - 1].wait_recv()
+    arrived(blk_all.at[pl.ds(0, 3)], xr_sem.at[4])
     plan_sums(blk_all, plan)
     plan_copy = pltpu.make_async_copy(plan, plan_s, w_sem.at[5])
     listed_copy = pltpu.make_async_copy(blk_all, listed, w_sem.at[6])
@@ -273,16 +283,12 @@
 
     relay_on(2)
     for d in (0, 1, 3, 2):
-        relay(d, 0).wait_recv()
-        relay(d, 1).wait_recv()
+        arrived(group_rows(seq_of(turn(x, -d), turn(y, 2), c)), rr_sem.at[d])
         cross(d, 2).start()
-    for d in (1, 2, 3):
-        x_copy(1, d).wait_recv()
+    arrived(qg_all.at[pl.ds(0, 3)], xr_sem.at[3])
     plan_copy.wait()
     listed_copy.wait()
-    for d in range(SIDE):
-        for k in range(SIDE):
-            cross(d, k).wait_recv()
+    arrived(kv_all.at[pl.ds(0, 64)], cr_sem.at[0])
 
     low = lax.broadcasted_iota(jnp.int32, (QB, QB), 1) < HDIM
     top = lax.broadcasted_iota(jnp.int32, (QB, QB), 0) < HDIM
@@ -304,7 +310,7 @@
     def bx_qa(d):
         to = turn(x, d)
         return remote(
-            dqa.at[to], bxr_qa.at[x], bxs_sem.at[1, d - 1], bxr_sem.at[1, d - 1], (seq_of(to, y, c), z)
+            dqa.at[to], bxr_qa.at[x], send.at[4], bxr_sem.at[3], (seq_of(to, y, c), z)
         )
 
     def step(i, carry):
@@ -334,51 +340,49 @@
         return seg[jnp.clip(plan_s[2, b], 0, QB)]
 
     def bcross(d, k):
-        return remote(dkv.at[d, k], side.at[d, k], bcs_sem.at[d, k], bcr_sem.at[d, k], sibling)
+        return remote(dkv.at[k, d], side.at[k, d], send.at[3], bcr_sem.at[k], sibling)
 
     def bx_kv(d):
         to = turn(x, d)
         return remote(
-            bxs_kv.at[to], bxr_kv.at[x], bxs_sem.at[0, d - 1], bxr_sem.at[0, d - 1], (seq_of(to, y, c), z)
+            bxs_kv.at[to], bxr_kv.at[x], send.at[3], bxr_sem.at[d - 1], (seq_of(to, y, c), z)
         )
 
     def bzk_copy(d, i):
         to, head = turn(z, d), turn(x, i)
         rows = pl.ds(pl.multiple_of(to * QB, QB), QB)
-        return remote(bzs_kv.at[head, rows], bzr_kv.at[z, head], bzk_s.at[d - 1, i], bzk_r.at[d - 1, i], (group, to))
+        return remote(bzs_kv.at[head, rows], bzr_kv.at[z, head], send.at[4], bzr_sem.at[0], (group, to))
 
     def bzq_copy(d):
         to = turn(z, d)
         rows = pl.ds(pl.multiple_of(to * QB, QB), QB)
-        return remote(bzs_qa.at[rows], bzr_qa.at[z], bzs_sem.at[d - 1], bzr_sem.at[d - 1], (group, to))
+        return remote(bzs_qa.at[rows], bzr_qa.at[z], send.at[4], bzr_sem.at[1], (group, to))
 
     def opposite(d, k):
         half = pl.ds(2 * k, 2)
         return remote(
-            opp.at[d, half], opp.at[SIDE + d, half], bys_sem.at[d, k], byr_sem.at[d, k],
+            opp.at[d, half], opp.at[SIDE + d, half], send.at[3], byr_sem.at[d],
             (seq_of(x, turn(y, (1, 3)[k]), c), z),
         )
 
     def beside(d, k):
         return remote(
-            y_send.at[d, k], y_recv.at[d, k], bys_sem.at[d, 2 + k], byr_sem.at[d, 2 + k],
+            y_send.at[d, k], y_recv.at[d, k], send.at[3], byr_sem.at[SIDE + d],
             (seq_of(x, turn(y, (1, 3)[k]), c), z),
         )
 
     def paired(d, k, n):
-        return partial_sum(seq_of(turn(x, d), turn(y, k), c), n) + side[d, k, n].astype(F32)
+        return partial_sum(seq_of(turn(x, d), turn(y, k), c), n) + side[k, d, n].astype(F32)
 
     def to_opposite(d):
-        bcross(d, 2).wait_recv()
         for n in range(4):
             opp[d, n] = paired(d, 2, n).astype(BF)
         opposite(d, 0).start()
         opposite(d, 1).start()
 
     def to_neighbours(d):
+        arrived(opp.at[SIDE + d], byr_sem.at[d])
         for k in range(2):
-            bcross(d, (1, 3)[k]).wait_recv()
-            opposite(d, k).wait_recv()
             for n in range(4):
                 total = paired(d, (1, 3)[k], n)
                 if n // 2 == k:
@@ -387,9 +391,7 @@
             beside(d, k).start()
 
     def settle(d):
-        bcross(d, 0).wait_recv()
-        for k in range(2):
-            beside(d, k).wait_recv()
+        arrived(y_recv.at[d], byr_sem.at[SIDE + d])
         for n in range(4):
             total = paired(d, 0, n) + (y_recv[d, 0, n].astype(F32) + y_recv[d, 1, n].astype(F32))
             rows = slice(QB * n, QB * n + QB)
@@ -412,40 +414,41 @@
     def w_x(d):
         return remote(
             wx_send.at[turn(x, d)], wx_recv.at[d - 1],
-            ws_sem.at[d], wr_sem.at[d], (seq_of(turn(x, d), y, c), z),
+            send.at[4], wr_sem.at[1], (seq_of(turn(x, d), y, c), z),
         )
 
     def w_y(d):
         return remote(
             wy_send.at[turn(y, d)], wy_recv.at[d - 1],
-            ws_sem.at[3 + d], wr_sem.at[3 + d], (seq_of(x, turn(y, d), c), z),
+            send.at[4], wr_sem.at[2], (seq_of(x, turn(y, d), c), z),
         )
 
     def w_z(d):
         return remote(
-            wz_send.at[turn(z, d)], wz_recv.at[z], ws_sem.at[6 + d], wr_sem.at[6 + d], (group, turn(z, d))
+            wz_send.at[turn(z, d)], wz_recv.at[z], send.at[5], wr_sem.at[3], (group, turn(z, d))
         )
 
     for k in (2, 1, 3, 0):
         for d in order:
             for n in range(4):
-                dkv[d, k, n] = partial_sum(seq_of(turn(x, d), turn(y, k), 1 - c), n).astype(BF)
+                dkv[k, d, n] = partial_sum(seq_of(turn(x, d), turn(y, k), 1 - c), n).astype(BF)
             bcross(d, k).start()
+    arrived(side.at[2], bcr_sem.at[2])
     for d in order:
         to_opposite(d)
+    arrived(side.at[1], bcr_sem.at[1])
+    arrived(side.at[3], bcr_sem.at[3])
     for d in order:
         to_neighbours(d)
 
-    for d in (1, 2, 3):
-        bx_qa(d).wait_recv()
+    arrived(bxr_qa.at[pl.ds(0, 3)], bxr_sem.at[3])
     for h in range(SIDE):
         bzs_qa[:, 128 * h : 128 * h + 128] = dot(place_hits[...], bxr_qa[h]).astype(BF)
     for d in (2, 1, 3):
         bzq_copy(d).start()
     bzr_qa[z] = bzs_qa[own_rows]
 
-    for d in (1, 2, 3):
-        z_copy(1, d).wait_recv()
+    arrived(go_all.at[pl.ds(0, 3 * QB)], zr_sem.at[1])
     group_mixed = []
     for half in range(2):
         a = bzs_qa[:, 256 * half : 256 * half + 128].astype(F32)
@@ -455,27 +458,15 @@
     for i in range(SIDE):
         part = dot(go_all[:, 256 * i : 256 * i + 256], group_mixed, 0, 0)
         wpart[4 * i : 4 * i + 4] = part.reshape(4, 2, 32, 256)
-    w_cross = remote(wc_send, wc_recv, ws_sem.at[0], wr_sem.at[0], sibling)
+    w_cross = remote(wc_send, wc_recv, send.at[4], wr_sem.at[0], sibling)
     wc_send[...] = wpart[:, 1 - c].astype(BF)
     w_cross.start()
 
-    for d in (1, 2, 3):
-        x_copy(0, d).wait_send()
-        x_copy(1, d).wait_send()
-        z_copy(0, d).wait_send()
-        z_copy(1, d).wait_send()
-        bx_qa(d).wait_send()
-        blk_copies[d - 1].wait_send()
-        for i in range(SIDE):
-            zk_copy(d, i).wait_send()
-    for d in range(SIDE):
-        for k in range(2):
-            y_copy(d, k).wait_send()
-            relay(d, k).wait_send()
-            opposite(d, k).wait_send()
-        for k in range(SIDE):
-            cross(d, k).wait_send()
-            bcross(d, k).wait_send()
+    sent(60, 0)
+    sent(124, 1)
+    blocks_sent = blk_all.at[pl.ds(0, 3)]
+    remote(blocks_sent, blocks_sent, send.at[2], xr_sem.at[4], sibling).wait_send()
+    arrived(side.at[0], bcr_sem.at[0])
 
     settle(2)
     settle(1)
@@ -492,15 +483,14 @@
     settle_z(1)
 
     wrows = wx_send[x].astype(F32)
+    arrived(wx_recv, wr_sem.at[1])
     for d in (1, 2, 3):
-        w_x(d).wait_recv()
         wrows += wx_recv[d - 1].astype(F32)
     wy_send[...] = wrows.reshape(SIDE, 32, 256)
     for d in (2, 1, 3):
         w_y(d).start()
 
-    for d in (1, 2, 3):
-        bzq_copy(d).wait_recv()
+    arrived(bzr_qa.at[pl.ds(0, 3)], bzr_sem.at[1])
     for h in range(SIDE):
         for half in range(2):
             a = bzr_qa[h, :, 256 * half : 256 * half + 128].astype(F32)
@@ -515,17 +505,15 @@
         gacc[:, rows] = dot(gproj[:, :1024], wbuf[rows, :1024], 1, 1)
 
     wrows = wy_send[y]
+    arrived(wy_recv, wr_sem.at[2])
     for d in (1, 2, 3):
-        w_y(d).wait_recv()
         wrows += wy_recv[d - 1]
     wz_send[...] = wrows.reshape(SIDE, 8, 256)
     for d in (2, 1, 3):
         w_z(d).start()
     wz_recv[z] = wz_send[z]
 
-    for i in range(SIDE):
-        for d in (1, 2, 3):
-            bzk_copy(d, i).wait_recv()
+    arrived(bzr_kv.at[pl.ds(0, 3)], bzr_sem.at[0])
     for h in range(SIDE):
         for half in range(2):
             a = bzr_kv[h, 2 * half].astype(F32)
@@ -538,23 +526,14 @@
         rows = slice(256 * i, 256 * i + 256)
         grad_nodes[:, rows] = (gacc[:, rows] + dot(gproj[:, 1024:], wbuf[rows, 1024:], 1, 1)).astype(BF)
 
-    for d in (1, 2, 3):
-        w_z(d).wait_recv()
+    arrived(wz_recv.at[pl.ds(0, 3)], wr_sem.at[3])
     for h in range(SIDE):
         w_grad[:, 256 * h : 256 * h + 256] = wz_recv[h]
 
-    w_cross.wait_send()
-    for d in (1, 2, 3):
-        bx_kv(d).wait_send()
-        bzq_copy(d).wait_send()
-        w_z(d).wait_send()
-        w_x(d).wait_send()
-        w_y(d).wait_send()
-        for i in range(SIDE):
-            bzk_copy(d, i).wait_send()
-    for d in range(SIDE):
-        for k in range(2):
-            beside(d, k).wait_send()
+    sent(124, 3)
+    sent(53, 4)
+    third = wz_send.at[pl.ds(0, 3)]
+    remote(third, third, send.at[5], wr_sem.at[3], sibling).wait_send()
 
 
 def hand_on(*refs):
@@ -601,10 +580,8 @@
             low(QB, 1024), low(QB, 3072), full(QB, 1024), full(16, 2, 32, 256), low(16, 32, 256), low(16, 32, 256),
             low(SIDE, QB, 256), low(3, QB, 256), full(SIDE, 32, 256), full(3, 32, 256),
             full(SIDE, 8, 256), full(SIDE, 8, 256),
-            dma(7), dma(3, 4), dma(3, 4), dma(2, 3), dma(2, 3), dma(3, 3), dma(3, 3),
-            dma(4, 4), dma(4, 4), dma(4, 4), dma(4, 4),
-            dma(3, 4), dma(3, 4), dma(3), dma(3), dma(2, 3), dma(2, 3),
-            dma(4, 4), dma(4, 4), dma(4, 4), dma(4, 4), dma(10), dma(10),
+            dma(7), dma(6), dma(4), dma(2), dma(5), dma(4, 2, 2), dma(4), dma(1),
+            dma(2), dma(4), dma(8), dma(4), dma(4),
         ],
         compiler_params=pltpu.CompilerParams(
             collective_id=0, has_side_effects=True, vmem_limit_bytes=VMEM_BYTES

time: 81.8 us -> 79.4 us (0.971)
  Pallas kernels: 81 us -> 78.6 us
    pallas_call x1, Pallas kernels: 79.1 us -> 76.7 us  [on_device(): pl.pallas_call(sublayer_kernel, out_shape=shapes, in_specs=[anywhere, any...]
where the time goes in v5:
time: 79.4 us; the launch traced here: 79.2 us
  Pallas kernels  78.6 us (99%)
    pallas_call x1, Pallas kernels, on_device(): pl.pallas_call(sublayer_kernel, out_shape=shapes, in_specs=[anywhere, any...  76.7 us
    pallas_call x1, Pallas kernels, on_device(): pl.pallas_call(hand_on, out_shape=shapes, in_specs=[vm] * 3, out_specs=(v...  1.84 us

profile of v5, /device:TPU:0, one launch (start us, length us, event | category | flops | bytes accessed | tf_op | source)
XLA Modules:
  0.0 79.2 jit_solution(16318381405511902425)
XLA Ops:
  0.6 76.7 %sublayer.1 = (bf16[128,1024]{1,0:T(8,128)(2,1)}, bf16[128,1024]{1,0:T(8,128)(2,1)}, f32[8,1024]{1,0:T(8,128)}) custom-call(bf16[128,1024]{1,0:T(8,128)(2,1)} %nodes_in.1, bf16[1024,3072]{1,0:T(8,128)(2,1)} %w_qkv.1, bf16[1024,1024]{1,0:T(8,128)(2,1)} %w_out.1, bf16[128,1024]{1,0:T(8,128)(2,1)} %go_in.1, s32[1,512]{1,0:T(1,128)} %bitcast.1, s32[4,8]{1,0:T(4,128)} %blk.1), custom_call_target="tpu_custom_call" | custom-call | tf_op jit(solution)/shard_map/sublayer/pallas_call | solution.py:564
  77.4 1.8 %results.1 = (bf16[128,1024]{1,0:T(8,128)(2,1)}, bf16[128,1024]{1,0:T(8,128)(2,1)}, f32[8,1024]{1,0:T(8,128)}) custom-call(bf16[128,1024]{1,0:T(8,128)(2,1)} %get-tuple-element.6.refs_0_, bf16[128,1024]{1,0:T(8,128)(2,1)} %get-tuple-element.7.refs_1_, f32[8,1024]{1,0:T(8,128)} %get-tuple-element.8.refs_2_), custom_call_target="tpu_custom_call" | custom-call | tf_op jit(solution)/shard_map/results/pallas_call | solution.py:591

commit v6 on v5

--- a/solution.py
+++ b/solution.py
@@ -314,15 +314,16 @@
         )
 
     def step(i, carry):
-        pairs = [softmax_and_grad(i, u, keys.at[u]) for u in range(4)]
+        pairs = [softmax_and_grad(2 * i + u // 4, u % 4, keys.at[u]) for u in range(8)]
         for u, (both, pair) in enumerate(pairs):
             back = dot(keys[u], pair, 0, 0)
-            dqa[i, u * QB : (u + 1) * QB] = jnp.where(top, back[:, :QB] * scale, back[:, QB:]).T.astype(BF)
+            rows = slice(u % 4 * QB, u % 4 * QB + QB)
+            dqa[2 * i + u // 4, rows] = jnp.where(top, back[:, :QB] * scale, back[:, QB:]).T.astype(BF)
             made = dot(pair, both).astype(BF)
-            parts[pl.ds(pl.multiple_of(32 * i + 8 * u, 8), 8)] = made.reshape(8, QB, 128)
+            parts[pl.ds(pl.multiple_of(64 * i + 8 * u, 8), 8)] = made.reshape(8, QB, 128)
         return carry
 
-    lax.fori_loop(0, 4, step, 0)
+    lax.fori_loop(0, 2, step, 0)
     for d in (2, 1, 3):
         bx_qa(d).start()
     bxr_qa[x] = dqa[x]
@@ -572,7 +573,7 @@
             low(SIDE, 4, QB, 128), low(*heads), low(QB, QB, 128), low(*heads),
             pltpu.VMEM((SIDE, 8, 128), jnp.int32), low(GROUP, 1024),
             pltpu.VMEM((8, QB), jnp.int32), pltpu.VMEM((8, QB), jnp.int32), pltpu.SMEM((8, QB), jnp.int32), pltpu.SMEM((SIDE, 8, 128), jnp.int32),
-            low(4, 1024, 128), low(QB, QB, 128), full(QB + 1, QB, 128), low(*heads),
+            low(8, 1024, 128), low(QB, QB, 128), full(QB + 1, QB, 128), low(*heads),
             low(SIDE, SIDE, 4, QB, 128), low(SIDE, SIDE, 4, QB, 128), low(2 * SIDE, 4, QB, 128),
             low(SIDE, 2, 4, QB, 128), low(SIDE, 2, 4, QB, 128),
             low(*heads), low(*heads), low(*heads), low(*heads), low(SIDE, SIDE, QB, 128),

time: 79.4 us -> 78.9 us (level)
  no operation moved by 1% of the time
where the time goes in v6:
time: 78.9 us; the launch traced here: 78.8 us
  Pallas kernels  78.1 us (99%)
    pallas_call x1, Pallas kernels, on_device(): pl.pallas_call(sublayer_kernel, out_shape=shapes, in_specs=[anywhere, any...  76.3 us
    pallas_call x1, Pallas kernels, on_device(): pl.pallas_call(hand_on, out_shape=shapes, in_specs=[vm] * 3, out_specs=(v...  1.84 us

profile of v6, /device:TPU:0, one launch (start us, length us, event | category | flops | bytes accessed | tf_op | source)
XLA Modules:
  0.0 78.8 jit_solution(14986246421009732513)
XLA Ops:
  0.6 76.3 %sublayer.1 = (bf16[128,1024]{1,0:T(8,128)(2,1)}, bf16[128,1024]{1,0:T(8,128)(2,1)}, f32[8,1024]{1,0:T(8,128)}) custom-call(bf16[128,1024]{1,0:T(8,128)(2,1)} %nodes_in.1, bf16[1024,3072]{1,0:T(8,128)(2,1)} %w_qkv.1, bf16[1024,1024]{1,0:T(8,128)(2,1)} %w_out.1, bf16[128,1024]{1,0:T(8,128)(2,1)} %go_in.1, s32[1,512]{1,0:T(1,128)} %bitcast.1, s32[4,8]{1,0:T(4,128)} %blk.1), custom_call_target="tpu_custom_call" | custom-call | tf_op jit(solution)/shard_map/sublayer/pallas_call | solution.py:565
  76.9 1.8 %results.1 = (bf16[128,1024]{1,0:T(8,128)(2,1)}, bf16[128,1024]{1,0:T(8,128)(2,1)}, f32[8,1024]{1,0:T(8,128)}) custom-call(bf16[128,1024]{1,0:T(8,128)(2,1)} %get-tuple-element.6.refs_0_, bf16[128,1024]{1,0:T(8,128)(2,1)} %get-tuple-element.7.refs_1_, f32[8,1024]{1,0:T(8,128)} %get-tuple-element.8.refs_2_), custom_call_target="tpu_custom_call" | custom-call | tf_op jit(solution)/shard_map/results/pallas_call | solution.py:592

commit v7 on v6

--- a/solution.py
+++ b/solution.py
@@ -112,19 +112,22 @@
     group = seq_of(x, y, c)
     sibling = (seq_of(x, y, 1 - c), z)
     order = (2, 1, 3, 0)
-    kv_cols = pl.ds(1024, 2048)
-    loads = [
-        pltpu.make_async_copy(src, dst, w_sem.at[i])
-        for i, (src, dst) in enumerate((
-            (nodes_in, nodes),
-            (w_qkv.at[:, kv_cols], wbuf.at[:, kv_cols]),
-            (w_qkv.at[:, pl.ds(0, 1024)], wbuf.at[:, pl.ds(0, 1024)]),
-            (go_in, go),
-            (w_out, wobuf),
-        ))
+
+    def load(i, src, dst):
+        copy = pltpu.make_async_copy(src, dst, w_sem.at[i])
+        copy.start()
+        return copy
+
+    def load_cols(i, first, width):
+        cols = pl.ds(pl.multiple_of(first, 256), width)
+        return load(i, w_qkv.at[:, cols], wbuf.at[:, cols])
+
+    load_nodes = load(0, nodes_in, nodes)
+    load_kv = [
+        [load_cols(7 + 2 * i + j, 1024 * j + 1024 + 256 * turn(z, d), 256) for j in range(2)]
+        for i, d in enumerate(order)
     ]
-    for load in loads:
-        load.start()
+    loads = [load(1, go_in, go), load_cols(2, 0, 1024), load(3, w_out, wobuf)]
     ready = greet(x, y, c, z, (1, 2, 3))
     own_rows = pl.ds(pl.multiple_of(z * QB, QB), QB)
 
@@ -195,11 +198,12 @@
             y_copy(d, k, 1).wait_recv()
             cross(d, (1, 3)[k]).start()
 
-    loads[0].wait()
-    loads[1].wait()
-    for d in (2, 1, 3, 0):
+    load_nodes.wait()
+    for i, d in enumerate(order):
         to = turn(z, d)
         off = pl.multiple_of(to * 256, 256)
+        for copy in load_kv[i]:
+            copy.wait()
         k = dot(nodes[...], wbuf[:, pl.ds(1024 + off, 256)])
         v = dot(nodes[...], wbuf[:, pl.ds(2048 + off, 256)])
         if d == 2:
@@ -233,8 +237,8 @@
         copy.start()
     blk_all[x] = blk_pad[...]
 
-    for load in loads[2:]:
-        load.wait()
+    for copy in loads:
+        copy.wait()
     for d in (2, 1, 3, 0):
         to = turn(z, d)
         off = pl.multiple_of(to * 256, 256)
@@ -341,7 +345,7 @@
         return seg[jnp.clip(plan_s[2, b], 0, QB)]
 
     def bcross(d, k):
-        return remote(dkv.at[k, d], side.at[k, d], send.at[3], bcr_sem.at[k], sibling)
+        return remote(dkv.at[k, d], side.at[k, d], send.at[3], bcr_sem.at[SIDE + d if k == 2 else k], sibling)
 
     def bx_kv(d):
         to = turn(x, d)
@@ -434,8 +438,8 @@
             for n in range(4):
                 dkv[k, d, n] = partial_sum(seq_of(turn(x, d), turn(y, k), 1 - c), n).astype(BF)
             bcross(d, k).start()
-    arrived(side.at[2], bcr_sem.at[2])
     for d in order:
+        arrived(side.at[2, d], bcr_sem.at[SIDE + d])
         to_opposite(d)
     arrived(side.at[1], bcr_sem.at[1])
     arrived(side.at[3], bcr_sem.at[3])
@@ -581,8 +585,8 @@
             low(QB, 1024), low(QB, 3072), full(QB, 1024), full(16, 2, 32, 256), low(16, 32, 256), low(16, 32, 256),
             low(SIDE, QB, 256), low(3, QB, 256), full(SIDE, 32, 256), full(3, 32, 256),
             full(SIDE, 8, 256), full(SIDE, 8, 256),
-            dma(7), dma(6), dma(4), dma(2), dma(5), dma(4, 2, 2), dma(4), dma(1),
-            dma(2), dma(4), dma(8), dma(4), dma(4),
+            dma(15), dma(6), dma(4), dma(2), dma(5), dma(4, 2, 2), dma(4), dma(1),
+            dma(2), dma(4), dma(8), dma(8), dma(4),
         ],
         compiler_params=pltpu.CompilerParams(
             collective_id=0, has_side_effects=True, vmem_limit_bytes=VMEM_BYTES

time: 78.9 us -> 78.3 us (level)
  no operation moved by 1% of the time
where the time goes in v7:
time: 78.3 us; the launch traced here: 78.2 us
  Pallas kernels  77.5 us (99%)
    pallas_call x1, Pallas kernels, on_device(): pl.pallas_call(sublayer_kernel, out_shape=shapes, in_specs=[anywhere, any...  75.7 us
    pallas_call x1, Pallas kernels, on_device(): pl.pallas_call(hand_on, out_shape=shapes, in_specs=[vm] * 3, out_specs=(v...  1.84 us

profile of v7, /device:TPU:0, one launch (start us, length us, event | category | flops | bytes accessed | tf_op | source)
XLA Modules:
  0.0 78.2 jit_solution(1314851582282158154)
XLA Ops:
  0.6 75.7 %sublayer.1 = (bf16[128,1024]{1,0:T(8,128)(2,1)}, bf16[128,1024]{1,0:T(8,128)(2,1)}, f32[8,1024]{1,0:T(8,128)}) custom-call(bf16[128,1024]{1,0:T(8,128)(2,1)} %nodes_in.1, bf16[1024,3072]{1,0:T(8,128)(2,1)} %w_qkv.1, bf16[1024,1024]{1,0:T(8,128)(2,1)} %w_out.1, bf16[128,1024]{1,0:T(8,128)(2,1)} %go_in.1, s32[1,512]{1,0:T(1,128)} %bitcast.1, s32[4,8]{1,0:T(4,128)} %blk.1), custom_call_target="tpu_custom_call" | custom-call | tf_op jit(solution)/shard_map/sublayer/pallas_call | solution.py:569
  76.3 1.8 %results.1 = (bf16[128,1024]{1,0:T(8,128)(2,1)}, bf16[128,1024]{1,0:T(8,128)(2,1)}, f32[8,1024]{1,0:T(8,128)}) custom-call(bf16[128,1024]{1,0:T(8,128)(2,1)} %get-tuple-element.6.refs_0_, bf16[128,1024]{1,0:T(8,128)(2,1)} %get-tuple-element.7.refs_1_, f32[8,1024]{1,0:T(8,128)} %get-tuple-element.8.refs_2_), custom_call_target="tpu_custom_call" | custom-call | tf_op jit(solution)/shard_map/results/pallas_call | solution.py:596
